TPU v7x, 128 devices: a whole 4x4x4 slice. The times are simulated.
128 devices in a mesh: member: 8 (over y, z_hi), domain: 16 (over z_lo, x, core).
Axes of the slice: x: 4, y: 4, z: 4 (z_hi: 2, z_lo: 2; z = z_hi * 2 + z_lo), core: 2. Of those that a mesh axis runs over, the one named last changes fastest.
Arguments:
- ensemble: float32 [80, 4, 3, 16, 4096], P('member', None, None, None, 'domain'), may hold values from -9 to 9
- velocity: float32 [2, 3, 16, 4096], P(None, None, None, 'domain'), may hold values from -0.5 to 0.5
- diffusivity: float32 [4], replicated, may hold values from 0.05 to 0.2
- land_mask: int32 [16, 4096], P(None, 'domain'), may hold values from 0 to 1
- obs_index: int32 [4, 8, 4], replicated, may hold values from 0 to 255, as said below
- obs_owner: int32 [4], replicated, may hold values from 0 to 127, as said below
- obs_value: float32 [4, 8], replicated, may hold values from -4 to 4
- obs_error: float32 [4, 8], replicated, may hold values from 0.2 to 1
Outputs:
- analysis: float32 [80, 4, 3, 16, 4096], P(None, None, None, 'member', 'domain')
Inputs may be any that keep to these rules, and one draw needn't show every extreme that they name: `obs_index`: each observed cell has land_mask 1. The first observation of batch 0 is field 0, level 0 at its block's first row and column; the last observation of batch 3 is field 3, level 2 at its block's last row and column. A device's number is its member index times the number of domain tiles plus its domain index. obs_owner[0] is the first device and obs_owner[3] the last.
All inputs are finite; a program needn't handle non-finite values.
Results may differ from a plain program's by a relative error of at most 0.0001.
Values sent between devices are 32-bit elements; how exact they have to be, the bound alone decides.
A program may use at most 192 MiB of HBM per device.

v0:
```python
import jax
import jax.numpy as jnp
from jax import lax
from jax.sharding import PartitionSpec as P

LOC_RADIUS = 64


def padded_2(array, sides, width):
    for axis, dim in sides:
        size, length = (lax.axis_size(axis), array.shape[dim])
        up = [(i, (i + 1) % size) for i in range(size)]
        down = [(j, i) for i, j in up]
        last = lax.slice_in_dim(array, length - width, length, axis=dim)
        initial = lax.slice_in_dim(array, 0, width, axis=dim)
        before = lax.ppermute(last, axis, up)
        after = lax.ppermute(initial, axis, down)
        array = jnp.concatenate([before, array, after], axis=dim)
    return array


def broadcast(value, axis, source):
    kept = jnp.where(lax.axis_index(axis) == source, value, 0).astype(value.dtype)
    return lax.psum(kept, axis)


def gaspari(distance, loc_radius):
    scaled = distance / loc_radius
    scaled_safe = jnp.maximum(scaled, 1.0)
    near_part = (
        ((-0.25 * scaled + 0.5) * scaled + 0.625) * scaled - 5.0 / 3.0
    ) * scaled * scaled + 1.0
    far_part = (
        ((((scaled / 12.0 - 0.5) * scaled + 0.625) * scaled + 5.0 / 3.0) * scaled - 5.0) * scaled
        + 4.0
        - 2.0 / (3.0 * scaled_safe)
    )
    return jnp.where(scaled <= 1.0, near_part, jnp.where(scaled < 2.0, far_part, 0.0))


def separation(row_from, col_from, row_to, col_to, grid_width):
    col_gap = jnp.abs(col_from - col_to)
    col_gap = jnp.minimum(col_gap, grid_width - col_gap)
    row_gap = row_from - row_to
    return jnp.sqrt((col_gap * col_gap + row_gap * row_gap).astype(jnp.float32))


def advance(center, col_next, col_prev, row_next, row_prev, flow_u, flow_v, diffuse, wet_part):
    tendency = (
        -flow_u * (col_next - col_prev) * 0.5
        - flow_v * (row_next - row_prev) * 0.5
        + diffuse * (col_next + col_prev + row_next + row_prev - 4.0 * center)
    )
    return wet_part * (center + tendency)


def regroup(member_state):
    return lax.all_to_all(member_state, "member", split_axis=3, concat_axis=0, tiled=True)


def increment_sums(change_flat, wet_cells, levels_total, members):
    per_cell = jnp.sum(change_flat.reshape(members, levels_total, -1), axis=0)
    local_sum = jnp.sum(per_cell * wet_cells[None, :], axis=1)
    return lax.psum((local_sum, jnp.sum(wet_cells)), ("member", "domain"))


def local(ensemble, velocity, diffusivity, land_mask, obs_index, obs_owner, obs_value, obs_error):
    fields = diffusivity.shape[0]
    levels = velocity.shape[1]
    levels_total = fields * levels
    diffuse = diffusivity[None, :, None, None, None]
    domain_count = lax.axis_size("domain")
    wet_all = land_mask.astype(jnp.float32)
    padded = padded_2(ensemble, (("domain", 4),), 1)
    zero_row = jnp.zeros_like(ensemble[:, :, :, :1, :])
    row_next = jnp.concatenate([ensemble[:, :, :, 1:, :], zero_row], axis=3)
    row_prev = jnp.concatenate([zero_row, ensemble[:, :, :, :-1, :]], axis=3)
    stepped = advance(
        ensemble,
        padded[..., 2:],
        padded[..., :-2],
        row_next,
        row_prev,
        velocity[0][None, None],
        velocity[1][None, None],
        diffuse,
        wet_all,
    )
    current = regroup(stepped)
    row_count = current.shape[3]
    first_row = lax.axis_index("member") * row_count
    wet_rows = lax.dynamic_slice_in_dim(wet_all, first_row, row_count, 0)
    members = current.shape[0]
    col_count = current.shape[4]
    grid_width = col_count * domain_count
    loc_radius = float(LOC_RADIUS)
    first_col = lax.axis_index("domain") * col_count
    grid_rows = first_row + jnp.arange(row_count, dtype=jnp.int32)[:, None]
    grid_cols = first_col + jnp.arange(col_count, dtype=jnp.int32)[None, :]
    wet_cells = wet_rows.reshape(-1)
    wet_flat = jnp.broadcast_to(wet_rows[None], (levels_total, row_count, col_count)).reshape(-1)
    flat_state = current.reshape(members, -1)
    spread = jnp.float32(members - 1)
    for batch_num in range(obs_owner.shape[0]):
        obs_slot = obs_index[batch_num]
        owner_dev = obs_owner[batch_num]
        level_of = obs_slot[:, 0] * levels + obs_slot[:, 1]
        position = (level_of * row_count + obs_slot[:, 2]) * col_count + obs_slot[:, 3]
        own_priors = jnp.take(flat_state, position, axis=1).T
        priors = broadcast(own_priors, ("member", "domain"), owner_dev)
        obs_rows = owner_dev // domain_count * row_count + obs_slot[:, 2]
        obs_cols = owner_dev % domain_count * col_count + obs_slot[:, 3]
        mutual = gaspari(
            separation(
                obs_rows[:, None],
                obs_cols[:, None],
                obs_rows[None, :],
                obs_cols[None, :],
                grid_width,
            ),
            loc_radius,
        )
        before = flat_state
        for obs_num in range(priors.shape[0]):
            prior_row = priors[obs_num]
            mean_prior = jnp.mean(prior_row)
            anomaly = prior_row - mean_prior
            obs_var = obs_error[batch_num, obs_num]
            denominator = jnp.sum(anomaly * anomaly) / spread + obs_var
            shrink = 1.0 / (1.0 + jnp.sqrt(obs_var / denominator))
            weight = obs_value[batch_num, obs_num] - mean_prior - shrink * anomaly
            taper = gaspari(
                separation(grid_rows, grid_cols, obs_rows[obs_num], obs_cols[obs_num], grid_width),
                loc_radius,
            )
            taper_flat = (
                jnp.broadcast_to(taper[None], (levels_total, row_count, col_count)).reshape(-1)
                * wet_flat
            )
            covariance = jnp.dot(anomaly, flat_state, precision=lax.Precision.HIGHEST)
            kalman = taper_flat * covariance / (spread * denominator)
            flat_state = flat_state + weight[:, None] * kalman[None, :]
            prior_cov = jnp.dot(priors, anomaly, precision=lax.Precision.HIGHEST)
            priors = (
                priors
                + (mutual[obs_num] * prior_cov / (spread * denominator))[:, None] * weight[None, :]
            )
        total_inc, wet_count = increment_sums(flat_state - before, wet_cells, levels_total, members)
        offset = total_inc / (members * wet_count)
        flat_state = (
            flat_state.reshape(members, levels_total, -1)
            - offset[None, :, None] * wet_cells[None, None, :]
        ).reshape(members, -1)
    return flat_state.reshape(members, fields, levels, row_count, col_count)


def solution(mesh):
    in_specs = (
        P("member", None, None, None, "domain"),
        P(None, None, None, "domain"),
        P(),
        P(None, "domain"),
        P(),
        P(),
        P(),
        P(),
    )
    out_specs = P(None, None, None, "member", "domain")
    return jax.shard_map(local, mesh=mesh, in_specs=in_specs, out_specs=out_specs, check_vma=False)
```

profile of v0, /device:TPU:1, one launch (start us, length us, event | category | flops | bytes accessed | tf_op | source)
XLA Modules:
  0.0 1767.2 jit_solution(16837437201812268285)
XLA Ops:
  101.9 6.9 add_multiply_fusion
  109.0 7.9 all-to-all-start
  175.3 68.9 %psum.72 = f32[8,80]{1,0:T(8,128)S(1)} all-reduce(f32[8,80]{1,0:T(8,128)S(1)} %fusion.92), channel_id=1, replica_groups=mesh['member'=8,'domain'=16] {'member','domain'}, use_global_device_ids=true, to_apply=%region_0.0 | all-reduce | flops 640 | bytes 5120 | tf_op jit(solution)/shard_map/psum | solution.py:24
  328.8 4.5 multiply_add_fusion.26
  340.0 5.3 multiply_add_fusion.25
  351.7 5.5 multiply_add_fusion.24
  365.0 5.9 subtract_reduce_fusion.3
  372.4 63.1 %all-reduce.2 = (f32[12]{0:T(128)}, f32[]{:T(128)}) all-reduce(f32[12]{0:T(128)S(1)} %reduce_sum.695, f32[]{:T(128)} %get-tuple-element.181), channel_id=1, replica_groups=mesh['member'=8,'domain'=16] {'member','domain'}, use_global_device_ids=true, to_apply=%region_19.21 | all-reduce | flops 13 | bytes 104 | tf_op jit(solution)/shard_map/psum | solution.py:64
  448.3 64.1 %psum.75 = f32[8,80]{1,0:T(8,128)S(1)} all-reduce(f32[8,80]{1,0:T(8,128)S(1)} %fusion.91), channel_id=1, replica_groups=mesh['member'=8,'domain'=16] {'member','domain'}, use_global_device_ids=true, to_apply=%region_22.24 | all-reduce | flops 640 | bytes 5120 | tf_op jit(solution)/shard_map/psum | solution.py:24
  556.6 6.5 fusion.62
  569.5 7.1 multiply_add_fusion.22
  583.1 7.9 multiply_add_fusion.21
  597.5 8.2 multiply_add_fusion.20
  612.1 9.1 multiply_add_fusion.19
  621.3 4.2 add.5659
  629.5 9.7 multiply_add_fusion.18
  647.0 11.4 multiply_add_fusion.17
  666.4 11.9 multiply_add_fusion.16
  687.1 11.8 subtract_reduce_fusion.2
  702.0 62.5 %psum.76 = f32[12]{0:T(128)} all-reduce(f32[12]{0:T(128)} %reduce_sum.715), channel_id=1, replica_groups=mesh['member'=8,'domain'=16] {'member','domain'}, use_global_device_ids=true, to_apply=%region_41.43 | all-reduce | flops 12 | bytes 96 | tf_op jit(solution)/shard_map/psum | solution.py:64
  766.6 5.5 add_subtract_fusion.2
  780.0 64.1 %psum.77 = f32[8,80]{1,0:T(8,128)} all-reduce(f32[8,80]{1,0:T(8,128)} %fusion.90), channel_id=1, replica_groups=mesh['member'=8,'domain'=16] {'member','domain'}, use_global_device_ids=true, to_apply=%region_42.44 | all-reduce | flops 640 | bytes 5120 | tf_op jit(solution)/shard_map/psum | solution.py:24
  936.0 13.4 fusion.63
  957.8 13.4 multiply_add_fusion.14
  979.6 14.2 multiply_add_fusion.13
  1002.1 14.9 multiply_add_fusion.12
  1025.3 16.1 multiply_add_fusion.11
  1049.9 17.3 multiply_add_fusion.10
  1067.1 4.2 add.5818
  1075.9 17.0 multiply_add_fusion.9
  1101.3 17.9 %multiply_add_fusion.8 = f32[8,10,4,3,2,256]{5,4,3,2,1,0:T(2,128)} fusion(f32[4,3,2,256]{3,2,1,0:T(2,128)} %mul.8417, f32[8,10]{1,0:T(8,128)} %sub.3713, f32[4,3,2,256]{3,2,1,0:T(2,128)} %mul.8384, f32[8,10]{1,0:T(8,128)} %sub.3694, f32[4,3,2,256]{3,2,1,0:T(2,128)} %mul.8351, f32[8,10]{1,0:T(8,128)} %sub.3676, f32[4,3,2,256]{3,2,1,0:T(2,128)} %mul.8318, ...), kind=kLoop, calls=%fused_computation.26 | loop fusion | flops 23592960 | bytes 4553920 | tf_op jit(solution)/shard_map/add | solution.py:142
  1127.7 16.9 subtract_reduce_fusion.1
  1147.8 62.5 %psum.78 = f32[12]{0:T(128)} all-reduce(f32[12]{0:T(128)} %reduce_sum.734), channel_id=1, replica_groups=mesh['member'=8,'domain'=16] {'member','domain'}, use_global_device_ids=true, to_apply=%region_61.63 | all-reduce | flops 12 | bytes 96 | tf_op jit(solution)/shard_map/psum | solution.py:64
  1211.8 7.4 add_subtract_fusion.1
  1227.0 64.2 %psum.79 = f32[8,80]{1,0:T(8,128)} all-reduce(f32[8,80]{1,0:T(8,128)} %fusion.89), channel_id=1, replica_groups=mesh['member'=8,'domain'=16] {'member','domain'}, use_global_device_ids=true, to_apply=%region_62.64 | all-reduce | flops 640 | bytes 5120 | tf_op jit(solution)/shard_map/psum | solution.py:24
  1384.9 19.9 %fusion.64 = f32[8,10,4,3,2,256]{5,4,3,2,1,0:T(2,128)} fusion(f32[4,3,2,256]{3,2,1,0:T(2,128)S(1)} %broadcast_multiply_fusion.1, f32[4,3,2,256]{3,2,1,0:T(2,128)} %mul.8450, f32[8,10]{1,0:T(8,128)} %sub.3714, f32[4,3,2,256]{3,2,1,0:T(2,128)} %mul.8417, f32[8,10]{1,0:T(8,128)} %sub.3713, f32[4,3,2,256]{3,2,1,0:T(2,128)} %mul.8384, f32[8,10]{1,0:T(8,128)} %sub.3694, ...), kind=kLoop, calls=%fused_computation.139 | loop fusion | flops 25067520 | bytes 4603392 | tf_op jit(solution)/shard_map/sub | solution.py:151
  1404.8 4.2 sub.3738
  1413.6 20.7 %multiply_add_fusion.6 = f32[8,10,4,3,2,256]{5,4,3,2,1,0:T(2,128)} fusion(f32[4,3,2,256]{3,2,1,0:T(2,128)} %mul.8512, f32[8,10]{1,0:T(8,128)} %sub.3769, f32[4,3,2,256]{3,2,1,0:T(2,128)} %copy-done.6, f32[4,3,2,256]{3,2,1,0:T(2,128)} %mul.8450, f32[8,10]{1,0:T(8,128)} %sub.3714, f32[4,3,2,256]{3,2,1,0:T(2,128)} %mul.8417, f32[8,10]{1,0:T(8,128)} %sub.3713, ...), kind=kLoop, calls=%fused_computation.22 | loop fusion | flops 26050560 | bytes 4628288 | tf_op jit(solution)/shard_map/add | solution.py:142
  1442.9 21.2 %multiply_add_fusion.5 = f32[8,10,4,3,2,256]{5,4,3,2,1,0:T(2,128)} fusion(f32[4,3,2,256]{3,2,1,0:T(2,128)} %mul.8557, f32[8,10]{1,0:T(8,128)} %sub.3787, f32[4,3,2,256]{3,2,1,0:T(2,128)} %mul.8512, f32[8,10]{1,0:T(8,128)} %sub.3769, f32[4,3,2,256]{3,2,1,0:T(2,128)} %copy-done.6, f32[4,3,2,256]{3,2,1,0:T(2,128)} %mul.8450, f32[8,10]{1,0:T(8,128)} %sub.3714, ...), kind=kLoop, calls=%fused_computation.21 | loop fusion | flops 27033600 | bytes 4653184 | tf_op jit(solution)/shard_map/add | solution.py:142
  1472.6 22.5 %multiply_add_fusion.4 = f32[8,10,4,3,2,256]{5,4,3,2,1,0:T(2,128)} fusion(f32[4,3,2,256]{3,2,1,0:T(2,128)} %mul.8590, f32[8,10]{1,0:T(8,128)} %sub.3805, f32[4,3,2,256]{3,2,1,0:T(2,128)} %mul.8557, f32[8,10]{1,0:T(8,128)} %sub.3787, f32[4,3,2,256]{3,2,1,0:T(2,128)} %mul.8512, f32[8,10]{1,0:T(8,128)} %sub.3769, f32[4,3,2,256]{3,2,1,0:T(2,128)} %copy-done.6, ...), kind=kLoop, calls=%fused_computation.20 | loop fusion | flops 28016640 | bytes 4678080 | tf_op jit(solution)/shard_map/add | solution.py:142
  1495.1 4.3 add.5932
  1504.0 23.7 %multiply_add_fusion.3 = f32[8,10,4,3,2,256]{5,4,3,2,1,0:T(2,128)} fusion(f32[4,3,2,256]{3,2,1,0:T(2,128)} %mul.8623, f32[8,10]{1,0:T(8,128)} %sub.3823, f32[4,3,2,256]{3,2,1,0:T(2,128)} %mul.8590, f32[8,10]{1,0:T(8,128)} %sub.3805, f32[4,3,2,256]{3,2,1,0:T(2,128)} %mul.8557, f32[8,10]{1,0:T(8,128)} %sub.3787, f32[4,3,2,256]{3,2,1,0:T(2,128)} %mul.8512, ...), kind=kLoop, calls=%fused_computation.19 | loop fusion | flops 28999680 | bytes 4702976 | tf_op jit(solution)/shard_map/add | solution.py:142
  1536.2 23.3 %multiply_add_fusion.2 = f32[8,10,4,3,2,256]{5,4,3,2,1,0:T(2,128)} fusion(f32[4,3,2,256]{3,2,1,0:T(2,128)} %mul.8656, f32[8,10]{1,0:T(8,128)} %sub.3841, f32[4,3,2,256]{3,2,1,0:T(2,128)} %mul.8623, f32[8,10]{1,0:T(8,128)} %sub.3823, f32[4,3,2,256]{3,2,1,0:T(2,128)} %mul.8590, f32[8,10]{1,0:T(8,128)} %sub.3805, f32[4,3,2,256]{3,2,1,0:T(2,128)} %mul.8557, ...), kind=kLoop, calls=%fused_computation.18 | loop fusion | flops 29982720 | bytes 4727872 | tf_op jit(solution)/shard_map/add | solution.py:142
  1568.0 27.6 %multiply_add_fusion.1 = f32[8,10,4,3,2,256]{5,4,3,2,1,0:T(2,128)} fusion(f32[4,3,2,256]{3,2,1,0:T(2,128)} %mul.8689, f32[8,10]{1,0:T(8,128)} %sub.3859, f32[4,3,2,256]{3,2,1,0:T(2,128)} %mul.8656, f32[8,10]{1,0:T(8,128)} %sub.3841, f32[4,3,2,256]{3,2,1,0:T(2,128)} %mul.8623, f32[8,10]{1,0:T(8,128)} %sub.3823, f32[4,3,2,256]{3,2,1,0:T(2,128)} %mul.8590, ...), kind=kLoop, calls=%fused_computation.17 | loop fusion | flops 30965760 | bytes 4752768 | tf_op jit(solution)/shard_map/add | solution.py:142
  1604.1 28.8 %multiply_add_fusion = f32[8,10,4,3,2,256]{5,4,3,2,1,0:T(2,128)} fusion(f32[4,3,2,256]{3,2,1,0:T(2,128)} %mul.8722, f32[8,10]{1,0:T(8,128)} %sub.3878, f32[4,3,2,256]{3,2,1,0:T(2,128)} %mul.8689, f32[8,10]{1,0:T(8,128)} %sub.3859, f32[4,3,2,256]{3,2,1,0:T(2,128)} %mul.8656, f32[8,10]{1,0:T(8,128)} %sub.3841, f32[4,3,2,256]{3,2,1,0:T(2,128)} %mul.8623, ...), kind=kLoop, calls=%fused_computation.16 | loop fusion | flops 31948800 | bytes 4777664 | tf_op jit(solution)/shard_map/add | solution.py:142
  1641.5 29.0 %subtract_reduce_fusion = f32[4,3,2,256]{3,2,1,0:T(2,128)S(1)} fusion(f32[4,3,2,256]{3,2,1,0:T(2,128)} %mul.8755, f32[8,10]{1,0:T(8,128)} %sub.3879, f32[4,3,2,256]{3,2,1,0:T(2,128)} %mul.8722, f32[8,10]{1,0:T(8,128)} %sub.3878, f32[4,3,2,256]{3,2,1,0:T(2,128)} %mul.8689, f32[8,10]{1,0:T(8,128)} %sub.3859, f32[4,3,2,256]{3,2,1,0:T(2,128)} %mul.8656, ...), kind=kLoop, calls=%fused_computation.14 | loop fusion | flops 33908736 | bytes 2861056 | tf_op jit(solution)/shard_map/reduce_sum | solution.py:62
  1674.0 62.5 %psum.80 = f32[12]{0:T(128)S(1)} all-reduce(f32[12]{0:T(128)} %reduce_sum.753), channel_id=1, replica_groups=mesh['member'=8,'domain'=16] {'member','domain'}, use_global_device_ids=true, to_apply=%region_81.83 | all-reduce | flops 12 | bytes 96 | tf_op jit(solution)/shard_map/psum | solution.py:64
  1736.7 30.2 %add_subtract_fusion = f32[80,4,3,2,256]{4,3,2,1,0:T(2,128)} fusion(f32[10,4,3,8,2,256]{5,4,2,1,0,3:T(2,128)} %copy.71, f32[4,3,2,256]{3,2,1,0:T(2,128)S(1)} %broadcast_multiply_fusion, f32[4,3,2,256]{3,2,1,0:T(2,128)} %mul.8755, f32[4,3,2,256]{3,2,1,0:T(2,128)} %mul.8722, f32[4,3,2,256]{3,2,1,0:T(2,128)} %mul.8689, f32[4,3,2,256]{3,2,1,0:T(2,128)} %mul.8656, ...), kind=kLoop, calls=%fused_computation.15 | loop fusion | flops 33423360 | bytes 4827136 | tf_op jit(solution)/shard_map/sub | solution.py:151
  (869 shorter events, 599.2 us)
Async XLA Ops:
  3.0 92.9 %collective-permute-start = (f32[10,4,3,16,1]{3,0,4,2,1:T(8,128)S(1)}, f32[10,4,3,16,1]{3,0,4,2,1:T(8,128)S(1)}, u32[]{:S(2)}, u32[]{:S(2)}) collective-permute-start(f32[10,4,3,16,1]{3,0,4,2,1:T(8,128)S(1)} %copy.76), channel_id=1, source_target_pairs={{1,0},{2,1},{3,2},{4,3},{5,4},{6,5},{7,6},{8,7},{9,8},{10,9},{11,1... | collective-permute-start | bytes 23048 | tf_op jit(solution)/shard_map/ppermute | solution.py:17
  6.3 92.2 %collective-permute-start.1 = (f32[10,4,3,16,1]{3,0,4,2,1:T(8,128)}, f32[10,4,3,16,1]{3,0,4,2,1:T(8,128)}, u32[]{:S(2)}, u32[]{:S(2)}) collective-permute-start(f32[10,4,3,16,1]{3,0,4,2,1:T(8,128)} %copy.77), channel_id=1, source_target_pairs={{0,1},{1,2},{2,3},{3,4},{4,5},{5,6},{6,7},{7,8},{8,9},{9,10},{10,1... | collective-permute-start | bytes 23048 | tf_op jit(solution)/shard_map/ppermute | solution.py:16
  24.4 71.5 %copy-start.84 = (s32[8,1]{0,1:T(1,128)}, s32[8,1]{0,1:T(1,128)S(1)}, u32[]{:S(2)}) copy-start(s32[8,1]{0,1:T(1,128)S(1)} %get-tuple-element.333) | copy-start | bytes 100
  24.4 77.4 %copy-start.80 = (s32[8,1]{0,1:T(1,128)}, s32[8,1]{0,1:T(1,128)S(1)}, u32[]{:S(2)}) copy-start(s32[8,1]{0,1:T(1,128)S(1)} %get-tuple-element.195) | copy-start | bytes 100
  24.5 77.4 %copy-start.82 = (s32[8,1]{0,1:T(1,128)}, s32[8,1]{0,1:T(1,128)S(1)}, u32[]{:S(2)}) copy-start(s32[8,1]{0,1:T(1,128)S(1)} %get-tuple-element.332) | copy-start | bytes 100
  27.1 68.8 %copy-start.86 = (s32[8,1]{0,1:T(1,128)}, s32[8,1]{0,1:T(1,128)S(1)}, u32[]{:S(2)}) copy-start(s32[8,1]{0,1:T(1,128)S(1)} %get-tuple-element.185) | copy-start | bytes 100
  27.1 68.8 %copy-start.88 = (s32[8,1]{0,1:T(1,128)}, s32[8,1]{0,1:T(1,128)S(1)}, u32[]{:S(2)}) copy-start(s32[8,1]{0,1:T(1,128)S(1)} %get-tuple-element.186) | copy-start | bytes 100
  27.1 68.8 %copy-start.89 = (s32[8,1]{0,1:T(1,128)}, s32[8,1]{0,1:T(1,128)S(1)}, u32[]{:S(2)}) copy-start(s32[8,1]{0,1:T(1,128)S(1)} %get-tuple-element.334) | copy-start | bytes 100
  37.9 333.0 %copy-start.18 = (f32[2,256]{1,0:T(2,128)}, f32[2,256]{1,0:T(2,128)S(1)}, u32[]{:S(2)}) copy-start(f32[2,256]{1,0:T(2,128)S(1)} %get-tuple-element.11) | copy-start | bytes 6148
  108.9 18.4 %copy-start.41 = (f32[12,2,2,128]{3,2,1,0:T(2,128)S(1)}, f32[12,2,2,128]{3,2,1,0:T(2,128)}, u32[]{:S(2)}) copy-start(f32[12,2,2,128]{3,2,1,0:T(2,128)} %broadcast_bitcast_fusion.20) | copy-start | bytes 73732
  108.9 19.0 %copy-start.42 = (f32[12,2,2,128]{3,2,1,0:T(2,128)S(1)}, f32[12,2,2,128]{3,2,1,0:T(2,128)}, u32[]{:S(2)}) copy-start(f32[12,2,2,128]{3,2,1,0:T(2,128)} %broadcast_bitcast_fusion.19) | copy-start | bytes 73732
  108.9 19.6 %copy-start.46 = (f32[12,2,2,128]{3,2,1,0:T(2,128)S(1)}, f32[12,2,2,128]{3,2,1,0:T(2,128)}, u32[]{:S(2)}) copy-start(f32[12,2,2,128]{3,2,1,0:T(2,128)} %broadcast_bitcast_fusion.18) | copy-start | bytes 73732
  108.9 20.3 %copy-start.47 = (f32[12,2,2,128]{3,2,1,0:T(2,128)S(1)}, f32[12,2,2,128]{3,2,1,0:T(2,128)}, u32[]{:S(2)}) copy-start(f32[12,2,2,128]{3,2,1,0:T(2,128)} %broadcast_bitcast_fusion.17) | copy-start | bytes 73732
  108.9 47.4 %copy-start.30 = (f32[4,8]{1,0:T(4,128)S(1)}, f32[4,8]{1,0:T(4,128)}, u32[]{:S(2)}) copy-start(f32[4,8]{1,0:T(4,128)} %param.17) | copy-start | bytes 388
  108.9 48.1 %copy-start.31 = (f32[4,8]{1,0:T(4,128)S(1)}, f32[4,8]{1,0:T(4,128)}, u32[]{:S(2)}) copy-start(f32[4,8]{1,0:T(4,128)} %param.16) | copy-start | bytes 388
  108.9 51.0 %copy-start.87 = (s32[8,1]{0,1:T(1,128)S(1)}, s32[8,1]{0,1:T(1,128)}, u32[]{:S(2)}) copy-start(s32[8,1]{0,1:T(1,128)} %copy-done.86) | copy-start | bytes 100
  108.9 52.4 %copy-start.83 = (s32[8,1]{0,1:T(1,128)S(1)}, s32[8,1]{0,1:T(1,128)}, u32[]{:S(2)}) copy-start(s32[8,1]{0,1:T(1,128)} %copy-done.82) | copy-start | bytes 100
  108.9 52.4 %copy-start.85 = (s32[8,1]{0,1:T(1,128)S(1)}, s32[8,1]{0,1:T(1,128)}, u32[]{:S(2)}) copy-start(s32[8,1]{0,1:T(1,128)} %copy-done.84) | copy-start | bytes 100
  109.0 53.1 %copy-start.81 = (s32[8,1]{0,1:T(1,128)S(1)}, s32[8,1]{0,1:T(1,128)}, u32[]{:S(2)}) copy-start(s32[8,1]{0,1:T(1,128)} %copy-done.80) | copy-start | bytes 100
  109.0 53.8 %all-to-all-start = ((f32[10,4,3,16,256]{4,0,2,1,3:T(8,128)}), f32[10,4,3,16,256]{4,0,2,1,3:T(8,128)S(1)}, u32[]{:S(2)}, u32[]{:S(2)}) async-start(f32[10,4,3,16,256]{4,0,2,1,3:T(8,128)} %add_multiply_fusion), calls=%async_computation | async-start | bytes 6291456 | tf_op jit(solution)/shard_map/all_to_all | solution.py:58
  172.7 116.5 %copy-start.79 = (f32[12,2,2,128]{3,1,2,0:T(2,128)S(1)}, f32[12,2,2,128]{3,1,2,0:T(2,128)}, u32[]{:S(2)}) copy-start(f32[12,2,2,128]{3,1,2,0:T(2,128)} %copy.78) | copy-start | bytes 73732
  288.6 149.0 %copy-start.106 = (f32[80]{0:T(128)}, f32[80]{0:T(128)S(1)}, u32[]{:S(2)}) copy-start(f32[80]{0:T(128)S(1)} %get-tuple-element.296) | copy-start | bytes 964
  288.7 358.3 %copy-start.4 = (f32[8,10]{1,0:T(8,128)}, f32[8,10]{1,0:T(8,128)S(1)}, u32[]{:S(2)}) copy-start(f32[8,10]{1,0:T(8,128)S(1)} %sub.3384) | copy-start | bytes 964
  288.8 358.2 %copy-start.3 = (f32[8,10]{1,0:T(8,128)}, f32[8,10]{1,0:T(8,128)S(1)}, u32[]{:S(2)}) copy-start(f32[8,10]{1,0:T(8,128)S(1)} %sub.3383) | copy-start | bytes 964
  288.8 358.1 %copy-start.2 = (f32[8,10]{1,0:T(8,128)}, f32[8,10]{1,0:T(8,128)S(1)}, u32[]{:S(2)}) copy-start(f32[8,10]{1,0:T(8,128)S(1)} %sub.3364) | copy-start | bytes 964
  288.9 358.1 %copy-start.1 = (f32[8,10]{1,0:T(8,128)}, f32[8,10]{1,0:T(8,128)S(1)}, u32[]{:S(2)}) copy-start(f32[8,10]{1,0:T(8,128)S(1)} %sub.3346) | copy-start | bytes 964
  289.2 148.4 %copy-start.11 = (f32[6144]{0:T(1024)}, f32[6144]{0:T(1024)S(1)}, u32[]{:S(2)}) copy-start(f32[6144]{0:T(1024)S(1)} %multiply_divide_fusion.31) | copy-start | bytes 73732
  298.9 138.7 %copy-start.12 = (f32[6144]{0:T(1024)}, f32[6144]{0:T(1024)S(1)}, u32[]{:S(2)}) copy-start(f32[6144]{0:T(1024)S(1)} %multiply_divide_fusion.30) | copy-start | bytes 73732
  308.2 129.4 %copy-start.13 = (f32[6144]{0:T(1024)}, f32[6144]{0:T(1024)S(1)}, u32[]{:S(2)}) copy-start(f32[6144]{0:T(1024)S(1)} %multiply_divide_fusion.29) | copy-start | bytes 73732
  318.4 119.2 %copy-start.14 = (f32[6144]{0:T(1024)}, f32[6144]{0:T(1024)S(1)}, u32[]{:S(2)}) copy-start(f32[6144]{0:T(1024)S(1)} %multiply_divide_fusion.28) | copy-start | bytes 73732
  328.8 108.8 %copy-start.15 = (f32[6144]{0:T(1024)}, f32[6144]{0:T(1024)S(1)}, u32[]{:S(2)}) copy-start(f32[6144]{0:T(1024)S(1)} %multiply_divide_fusion.27) | copy-start | bytes 73732
  339.9 97.7 %copy-start.16 = (f32[6144]{0:T(1024)}, f32[6144]{0:T(1024)S(1)}, u32[]{:S(2)}) copy-start(f32[6144]{0:T(1024)S(1)} %multiply_divide_fusion.26) | copy-start | bytes 73732
  351.7 86.0 %copy-start.17 = (f32[6144]{0:T(1024)}, f32[6144]{0:T(1024)S(1)}, u32[]{:S(2)}) copy-start(f32[6144]{0:T(1024)S(1)} %multiply_divide_fusion.25) | copy-start | bytes 73732
  442.3 75.0 %copy-start.146 = (f32[8,8]{1,0:T(8,128)S(1)}, f32[8,8]{1,0:T(8,128)}, u32[]{:S(2)}) copy-start(f32[8,8]{1,0:T(8,128)} %fusion.76) | copy-start | bytes 772
  442.3 114.2 %copy-start.19 = (f32[2,256]{1,0:T(2,128)S(1)}, f32[2,256]{1,0:T(2,128)}, u32[]{:S(2)}) copy-start(f32[2,256]{1,0:T(2,128)} %copy-done.18) | copy-start | bytes 6148
  524.4 38.6 %copy-start.110 = (f32[1,80]{1,0:T(1,128)}, f32[1,80]{1,0:T(1,128)S(1)}, u32[]{:S(2)}) copy-start(f32[1,80]{1,0:T(1,128)S(1)} %get-tuple-element.57) | copy-start | bytes 964
  529.7 33.4 %copy-start.112 = (f32[1,80]{1,0:T(1,128)}, f32[1,80]{1,0:T(1,128)S(1)}, u32[]{:S(2)}) copy-start(f32[1,80]{1,0:T(1,128)S(1)} %get-tuple-element.55) | copy-start | bytes 964
  534.9 28.2 %copy-start.114 = (f32[1,80]{1,0:T(1,128)}, f32[1,80]{1,0:T(1,128)S(1)}, u32[]{:S(2)}) copy-start(f32[1,80]{1,0:T(1,128)S(1)} %get-tuple-element.53) | copy-start | bytes 964
  556.2 73.3 %copy-start.10 = (f32[8,10]{1,0:T(8,128)}, f32[8,10]{1,0:T(8,128)S(1)}, u32[]{:S(2)}) copy-start(f32[8,10]{1,0:T(8,128)S(1)} %sub.3511) | copy-start | bytes 964
  556.2 73.2 %copy-start.9 = (f32[8,10]{1,0:T(8,128)}, f32[8,10]{1,0:T(8,128)S(1)}, u32[]{:S(2)}) copy-start(f32[8,10]{1,0:T(8,128)S(1)} %sub.3493) | copy-start | bytes 964
  556.3 73.2 %copy-start.8 = (f32[8,10]{1,0:T(8,128)}, f32[8,10]{1,0:T(8,128)S(1)}, u32[]{:S(2)}) copy-start(f32[8,10]{1,0:T(8,128)S(1)} %sub.3475) | copy-start | bytes 964
  556.4 90.6 %copy-start.7 = (f32[8,10]{1,0:T(8,128)}, f32[8,10]{1,0:T(8,128)S(1)}, u32[]{:S(2)}) copy-start(f32[8,10]{1,0:T(8,128)S(1)} %sub.3457) | copy-start | bytes 964
  556.5 90.5 %copy-start.5 = (f32[8,10]{1,0:T(8,128)}, f32[8,10]{1,0:T(8,128)S(1)}, u32[]{:S(2)}) copy-start(f32[8,10]{1,0:T(8,128)S(1)} %sub.3439) | copy-start | bytes 964
  1641.5 29.0 %copy-start.22 = (f32[2,256]{1,0:T(2,128)S(1)}, f32[2,256]{1,0:T(2,128)}, u32[]{:S(2)}) copy-start(f32[2,256]{1,0:T(2,128)} %copy-done.18) | copy-start | bytes 6148
  1671.2 65.4 %copy-start.23 = (f32[2,256]{1,0:T(2,128)S(1)}, f32[2,256]{1,0:T(2,128)}, u32[]{:S(2)}) copy-start(f32[2,256]{1,0:T(2,128)} %copy-done.18) | copy-start | bytes 6148
  1671.2 65.5 %copy-start.107 = (f32[80]{0:T(128)S(1)}, f32[80]{0:T(128)}, u32[]{:S(2)}) copy-start(f32[80]{0:T(128)} %copy-done.106) | copy-start | bytes 964
  1671.2 65.5 %copy-start.108 = (f32[80]{0:T(128)S(1)}, f32[80]{0:T(128)}, u32[]{:S(2)}) copy-start(f32[80]{0:T(128)} %fusion.367) | copy-start | bytes 964
  1671.2 65.5 %copy-start.109 = (f32[80]{0:T(128)S(1)}, f32[80]{0:T(128)}, u32[]{:S(2)}) copy-start(f32[80]{0:T(128)} %fusion.362) | copy-start | bytes 964
  (110 other events, 452.7 us)
where the time goes:
time: 1790 us; the launch traced here: 1770 us
  other arithmetic  727 us (41%)
  blocking collectives  512 us (29%)
  local copies, waits for them, and re-layouts  303 us (17%)
  between operations  119 us (7%)
  matrix products  96.1 us (5%)
    add x28, other arithmetic, local(): flat_state = flat_state + weight[:, None] * kalman[None, :]  373 us
    psum x4, blocking collectives, broadcast(): return lax.psum(kept, axis)  261 us
    psum x4, blocking collectives, increment_sums(): return lax.psum((local_sum, jnp.sum(wet_cells)), ('member', 'domain'))  251 us
    add x28, local copies, waits for them, and re-layouts, local(): flat_state = flat_state + weight[:, None] * kalman[None, :]  110 us
    sub x7, other arithmetic, local(): flat_state.reshape(members, levels_total, -1)  87.1 us
    dot_general x32, matrix products, local(): covariance = jnp.dot(anomaly, flat_state, precision=lax.Precision.HIGHEST)  82.8 us
    unnamed x378, local copies, waits for them, and re-layouts  68.3 us
    reduce_sum x4, other arithmetic, increment_sums(): per_cell = jnp.sum(change_flat.reshape(members, levels_total, -1), axis=0)  63.6 us
  transfers between devices with their start and end apart: 3, of which 0 were waited for; matrix products, arithmetic and copies ran while one was open for 7% of the time, Pallas kernels for 0%

commit v1 on v0

v1 whole, which is shorter than its diff:
```python
import jax
import jax.numpy as jnp
from jax import lax
from jax.experimental import pallas as pl
from jax.experimental.pallas import tpu as pltpu
from jax.sharding import PartitionSpec as P

LOC_RADIUS = 64.0
MEM, DOM = 8, 16
MESH = pl.DeviceIdType.MESH
F32, BF16 = jnp.float32, jnp.bfloat16
HIGH = lax.Precision.HIGHEST


def gaspari(distance):
    scaled = distance * (1.0 / LOC_RADIUS)
    safe = jnp.maximum(scaled, 1.0)
    near = (((-0.25 * scaled + 0.5) * scaled + 0.625) * scaled - 5.0 / 3.0) * scaled * scaled + 1.0
    far = (
        ((((scaled * (1.0 / 12.0) - 0.5) * scaled + 0.625) * scaled + 5.0 / 3.0) * scaled - 5.0) * scaled
        + 4.0
        - (2.0 / 3.0) / safe
    )
    return jnp.where(scaled <= 1.0, near, jnp.where(scaled < 2.0, far, 0.0))


def separation(row_a, col_a, row_b, col_b):
    gap = jnp.abs(col_a - col_b)
    gap = jnp.minimum(gap, 4096 - gap)
    rows = row_a - row_b
    return jnp.sqrt((gap * gap + rows * rows).astype(F32))


def iota(shape, dim):
    return lax.broadcasted_iota(jnp.int32, shape, dim)


def halves(x):
    hi = x.astype(BF16)
    return hi, (x - hi.astype(F32)).astype(BF16)


def mm(a, b):
    return jnp.dot(a, b, preferred_element_type=F32)


def mm_nt(a, b, precision=None):
    return lax.dot_general(a, b, (((1,), (1,)), ((), ())), precision=precision, preferred_element_type=F32)


def kernel(
    ens, vel, mask, diff_in, oidx_in, oown_in, oval_in, oerr_in, x1_out, mrow_out,
    diff, oidx, oown, oval, oerr, E, V, W, F, D, eW, eE, pack, halo, vbuf, vin, Z, RB, TP, Pm, Zi, bcol, gcol, LB,
    L1h, L1l, L2h, L2l, Kf, Kh, Kl, sbuf, sin1, sin2,
    in_sem, loc_sem, out_sem, hs, hr, as_, ar, d1s, d1r, m1s, m1r, d2s, d2r, m2s, m2r,
):
    me, dom = lax.axis_index("member"), lax.axis_index("domain")

    small = ((vel, V), (mask, W), (diff_in, diff), (oidx_in, oidx), (oown_in, oown), (oval_in, oval), (oerr_in, oerr))
    small = [pltpu.make_async_copy(src, dst, in_sem.at[3 + i]) for i, (src, dst) in enumerate(small)]
    copies = []
    for g in range(3):
        copies.append(pltpu.make_async_copy(ens.at[:, pl.ds(4 * g, 4)], E.at[:, pl.ds(4 * g, 4)], in_sem.at[g]))
    for c in small + copies:
        c.start()
    barrier = pltpu.get_barrier_semaphore()
    for i in range(1, MEM):
        pl.semaphore_signal(barrier, inc=1, device_id={"member": lax.rem(me + i, MEM)}, device_id_type=MESH)
    for i in range(1, DOM):
        pl.semaphore_signal(barrier, inc=1, device_id={"domain": lax.rem(dom + i, DOM)}, device_id_type=MESH)
    for c in small:
        c.wait()

    wet = W[...].astype(F32)
    row, col = iota((16, 256), 0), iota((16, 256), 1)
    lane16 = iota((16, 128), 1)

    def interior(fl, acc):
        acc = list(acc)
        lev, fld = lax.rem(fl, 3), lax.div(fl, 3)
        u, v, d = V[0, lev], V[1, lev], diff[fld]
        cen = wet * (1.0 - 4.0 * d)
        east, west = wet * (d - 0.5 * u), wet * (d + 0.5 * u)
        north, south = wet * (d - 0.5 * v), wet * (d + 0.5 * v)
        eW[fl] = jnp.where(lane16 == 0, west[:, :128], 0.0)
        eE[fl] = jnp.where(lane16 == 127, east[:, 128:], 0.0)
        east, west = jnp.where(col == 255, 0.0, east), jnp.where(col == 0, 0.0, west)
        north, south = jnp.where(row == 15, 0.0, north), jnp.where(row == 0, 0.0, south)
        for m in range(10):
            x = E[m, fl]
            F[m, fl] = (
                cen * x
                + east * pltpu.roll(x, 255, 1)
                + west * pltpu.roll(x, 1, 1)
                + north * pltpu.roll(x, 15, 0)
                + south * pltpu.roll(x, 1, 0)
            )
            slot = 2 * ((m % 5) * 12 + fl)
            edges = pltpu.roll(jnp.where(lane16 == 0, x[:, :128], x[:, 128:]), slot, 1)
            here = (lane16 == slot) | (lane16 == jnp.bitwise_and(slot + 127, 127))
            acc[m // 5] = jnp.where(here, edges, acc[m // 5])
        return tuple(acc)

    acc = (jnp.zeros((16, 128), F32), jnp.zeros((16, 128), F32))
    for g in range(3):
        copies[g].wait()
        acc = lax.fori_loop(4 * g, 4 * g + 4, interior, acc)
    pack[0], pack[1] = acc[0], acc[1]

    lane32, sub32 = iota((32, 128), 1), iota((32, 128), 0)

    def wide_l(x, rows):
        return jnp.broadcast_to(x[0:1, :], (rows, 128))

    zi = jnp.zeros((32, 128), jnp.int32)
    row_s, col_s, fl_s, row_l, col_l, fl_l = zi, zi, zi, zi, zi, zi
    val_s = jnp.zeros((32, 128), F32)
    places = []
    for k in range(32):
        b, n = k // 8, k % 8
        own = oown[b]
        r = jnp.right_shift(own, 4) * 2 + oidx[b, 2, n]
        c = jnp.bitwise_and(own, 15) * 256 + oidx[b, 3, n]
        f = oidx[b, 0, n] * 3 + oidx[b, 1, n]
        places.append((r, c))
        row_s, col_s, fl_s = (jnp.where(sub32 == k, s, a) for s, a in ((r, row_s), (c, col_s), (f, fl_s)))
        row_l, col_l, fl_l = (jnp.where(lane32 == k, s, a) for s, a in ((r, row_l), (c, col_l), (f, fl_l)))
        val_s = jnp.where(sub32 == k, oval[b, n], val_s)
    rho = gaspari(separation(row_s, col_s, row_l, col_l))
    for k in range(32):
        RB[k] = jnp.broadcast_to(rho[:, k : k + 1], (32, 128))

    sub8, lane8 = iota((8, 256), 0), iota((8, 256), 1)
    odd = jnp.bitwise_and(sub8, 1) == 1
    wet0 = jnp.broadcast_to(W[pl.ds(2 * me, 1), :].astype(F32), (8, 256))
    wet1 = jnp.broadcast_to(W[pl.ds(2 * me + 1, 1), :].astype(F32), (8, 256))
    wet8 = jnp.where(odd, wet1, wet0)
    row8, col8 = 2 * me + jnp.bitwise_and(sub8, 1), dom * 256 + lane8
    for k in range(32):
        TP[k] = gaspari(separation(row8, col8, places[k][0], places[k][1])) * wet8

    pl.semaphore_wait(barrier, MEM + DOM - 2)

    right, left = lax.rem(dom + 1, DOM), lax.rem(dom + DOM - 1, DOM)
    sends = []

    def remote(src, dst, send, recv, where):
        c = pltpu.make_async_remote_copy(
            src_ref=src, dst_ref=dst, send_sem=send, recv_sem=recv, device_id=where, device_id_type=MESH
        )
        c.start()
        sends.append(c)
        return c

    to_left = remote(pack, halo.at[0], hs.at[0], hr.at[0], {"domain": left})
    to_right = remote(pack, halo.at[1], hs.at[1], hr.at[1], {"domain": right})
    to_left.wait_recv()
    to_right.wait_recv()
    even = jnp.bitwise_and(lane16, 1) == 0
    merged = [jnp.where(even, halo[0, h], pltpu.roll(halo[1, h], 2, 1)) for h in range(2)]

    def fix(fl, carry):
        west, east = eW[fl], eE[fl]
        for m in range(10):
            slot = 2 * ((m % 5) * 12 + fl)
            y = pltpu.roll(merged[m // 5], 127 - slot, 1)
            F[m, fl, :, 0:128] = F[m, fl, :, 0:128] + y * west
            F[m, fl, :, 128:256] = F[m, fl, :, 128:256] + y * east
        return carry

    arrivals, locals_ = [], []

    def scatter(g):
        fls = pl.ds(4 * g, 4)
        mine = D.at[pl.ds(10 * lax.div(me, 4), 10), fls, pl.ds(2 * lax.rem(me, 4), 2), :]
        c = pltpu.make_async_copy(F.at[:, fls, pl.ds(2 * me, 2), :], mine, loc_sem.at[g])
        c.start()
        locals_.append(c)
        for i in (4, 5, 3, 2, 6, 1, 7):
            t = lax.rem(me + i, MEM)
            arrivals.append(
                remote(F.at[:, fls, pl.ds(2 * t, 2), :], mine, as_.at[7 * g + i - 1], ar.at[7 * g + i - 1], {"member": t})
            )

    lax.fori_loop(0, 4, fix, 0)
    scatter(0)
    lax.fori_loop(4, 12, fix, 0)

    pick = (iota((256, 128), 0) + dom * 256 == wide_l(col_l, 256)) & (iota((256, 128), 1) < 32)
    pick = jnp.where(pick, 1.0, 0.0).astype(BF16)
    at_row = jnp.bitwise_and(iota((160, 128), 0), 15) == wide_l(row_l, 160)
    got = jnp.zeros((160, 128), F32)
    for fl in range(12):
        x = F[:, fl].reshape(160, 256)
        hi = x.astype(BF16)
        rest = x - hi.astype(F32)
        mid, lo = halves(rest)
        got = jnp.where(wide_l(fl_l, 160) == fl, mm(hi, pick) + (mm(mid, pick) + mm(lo, pick)), got)
    got = jnp.where(at_row, got, 0.0)
    vbuf[...] = jnp.zeros((16, 128), F32)
    vbuf[0:10, :] = jnp.sum(got.reshape(10, 16, 128), axis=1)
    tile_parts = [
        remote(vbuf, vin.at[i - 1], d1s.at[i - 1], d1r.at[i - 1], {"domain": lax.rem(dom + i, DOM)}) for i in range(1, DOM)
    ]
    scatter(1)
    scatter(2)
    total = vbuf[...]
    for i, c in enumerate(tile_parts):
        c.wait_recv()
        total = total + vin[i]
    Z[me] = total
    groups = [
        remote(Z.at[me], Z.at[me], m1s.at[i - 1], m1r.at[i - 1], {"member": lax.rem(me + i, MEM)}) for i in range(1, MEM)
    ]
    for c in groups:
        c.wait_recv()

    Y = jnp.transpose(Z[...].reshape(128, 128))[:32]
    real = jnp.bitwise_and(lane32, 15) < 10
    ybar = jnp.broadcast_to(jnp.sum(Y, axis=1, keepdims=True) * (1.0 / 80.0), (32, 128))
    A = jnp.where(real, Y - ybar, 0.0)
    inv = jnp.where(lane32 == sub32, 1.0, 0.0).astype(F32)
    for k in range(32):
        a, z = A[k : k + 1, :], inv[k : k + 1, :]
        cov = jnp.broadcast_to(jnp.sum(A * a, axis=1, keepdims=True), (32, 128))
        err = oerr[k // 8, k % 8]
        den = cov[k : k + 1, :] * (1.0 / 79.0) + err
        gain = 1.0 / (79.0 * den)
        beta = 1.0 / (1.0 + jnp.sqrt(err / den))
        Pm[k : k + 1, :] = a
        Zi[k : k + 1, :] = z
        bcol[k : k + 1, :] = beta
        gcol[k : k + 1, :] = gain
        step = RB[k] * cov * gain
        A = A - (step * beta) * a
        inv = inv - step * z

    Pv = Pm[...]
    Pb = Pv * bcol[...]
    low = mm_nt(Pv, Pb, HIGH)
    for j in range(31):
        LB[j] = jnp.broadcast_to(low[:, j : j + 1], (32, 128))
    for k in range(32):
        TP[k] = TP[k] * jnp.broadcast_to(gcol[k : k + 1, 0:1], (8, 256))

    n = iota((128, 640), 1)
    unit = jnp.right_shift(n, 5)
    q = jnp.bitwise_and(jnp.right_shift(n, 1), 3)
    upper = (unit >= 10).astype(jnp.int32)
    spread = jnp.where((4 * upper + q) * 16 + unit - 10 * upper == iota((128, 640), 0), 1.0, 0.0).astype(BF16)
    n = iota((8, 640), 1)
    match = jnp.bitwise_and(jnp.right_shift(n, 3), 3) * 2 + jnp.bitwise_and(n, 1) == iota((8, 640), 0)
    keep = jnp.broadcast_to(jnp.where(match, 1.0, 0.0)[None], (32, 8, 640))

    def kron(part):
        return (jnp.broadcast_to(mm(part, spread)[:, None, :], (32, 8, 640)) * keep).reshape(256, 640)

    hi, lo = halves(Pv)
    L1h[...] = kron(hi).astype(BF16)
    L1l[...] = kron(lo).astype(BF16)
    hi, lo = halves(Pb)
    L2h[...] = jnp.transpose(kron(hi)).astype(BF16)
    L2l[...] = jnp.transpose(kron(lo)).astype(BF16)
    invT = jnp.transpose(jnp.concatenate([Zi[...], jnp.zeros((96, 128), F32)], axis=0))[:32]

    sums = jnp.zeros((8, 256), F32)
    for g in range(3):
        locals_[g].wait()
        for c in arrivals[7 * g : 7 * g + 7]:
            c.wait_recv()
        xh, xl = halves(D[:, 4 * g : 4 * g + 4].reshape(640, 256))
        cov = mm(L1h[...], xh) + (mm(L1h[...], xl) + mm(L1l[...], xh))
        gains = []
        for k in range(32):
            left_, right_ = cov[8 * k : 8 * k + 8, :128], cov[8 * k : 8 * k + 8, 128:]
            for j in range(k):
                s = jnp.broadcast_to(LB[j, k : k + 1, :], (8, 128))
                left_, right_ = left_ - s * gains[j][0], right_ - s * gains[j][1]
            left_, right_ = left_ * TP[k, :, 0:128], right_ * TP[k, :, 128:256]
            gains.append((left_, right_))
            Kf[g, 8 * k : 8 * k + 8, 0:128] = left_
            Kf[g, 8 * k : 8 * k + 8, 128:256] = right_
        hi, lo = halves(Kf[g])
        Kh[g], Kl[g] = hi, lo
        pick = jnp.where(sub8 == g, 1.0, 0.0).astype(BF16)
        sums = sums + (mm_nt(pick, hi) + mm_nt(pick, lo))
    sbuf[0] = jnp.where(sub8 == 3, wet0 + wet1, sums)
    parts = [
        remote(sbuf.at[0], sin1.at[i - 1], d2s.at[i - 1], d2r.at[i - 1], {"domain": lax.rem(dom + i, DOM)})
        for i in range(1, DOM)
    ]

    outs = []

    def update(g):
        change = mm(L2h[...], Kh[g]) + (mm(L2h[...], Kl[g]) + mm(L2l[...], Kh[g]))
        D[:, 4 * g : 4 * g + 4] = D[:, 4 * g : 4 * g + 4] - change.reshape(20, 4, 8, 256)
        for s in range(8):
            c = pltpu.make_async_copy(
                D.at[pl.ds(10 * (s // 4), 10), pl.ds(4 * g, 4), pl.ds(2 * (s % 4), 2), :],
                x1_out.at[pl.ds(10 * s, 10), pl.ds(4 * g, 4), :, :],
                out_sem.at[8 * g + s],
            )
            c.start()
            outs.append(c)

    update(0)
    update(1)
    total = sbuf[0]
    for i, c in enumerate(parts):
        c.wait_recv()
        total = total + sin1[i]
    sbuf[1] = total
    parts = [
        remote(sbuf.at[1], sin2.at[i - 1], m2s.at[i - 1], m2r.at[i - 1], {"member": lax.rem(me + i, MEM)})
        for i in range(1, MEM)
    ]
    update(2)
    for i, c in enumerate(parts):
        c.wait_recv()
        total = total + sin2[i]

    cells = jnp.sum(jnp.sum(jnp.where(sub8 == 3, total, 0.0), axis=1, keepdims=True), axis=0, keepdims=True)
    share = total * (1.0 / jnp.broadcast_to(cells, (8, 256)))
    fl_w = jnp.concatenate([fl_s, fl_s], axis=1)
    picked = jnp.zeros((32, 256), F32)
    for g in range(3):
        picked = jnp.where(jnp.right_shift(fl_w, 2) == g, share[g : g + 1, :], picked)
    four = jnp.bitwise_and(jnp.right_shift(iota((32, 256), 1), 1), 3)
    picked = jnp.where(four == jnp.bitwise_and(fl_w, 3), picked, 0.0)
    fold = jnp.where(jnp.right_shift(iota((256, 128), 0), 3) == iota((256, 128), 1), 1.0, 0.0).astype(BF16)
    hi, lo = halves(picked)
    shifts = mm(hi, fold) + mm(lo, fold)
    shifts = jnp.where(jnp.right_shift(lane32, 3) < jnp.right_shift(sub32, 3), shifts, 0.0)
    base = val_s - ybar
    innov = jnp.sum(invT * base, axis=0, keepdims=True)
    for _ in range(3):
        moved = base + jnp.sum(shifts * innov, axis=1, keepdims=True)
        innov = jnp.sum(invT * moved, axis=0, keepdims=True)
    wide = jnp.zeros((8, 256), F32)
    mean = [jnp.zeros((8, 256), F32) for _ in range(3)]
    for k in range(32):
        dk = jnp.broadcast_to(innov[0:1, k : k + 1], (8, 256))
        wide = jnp.where(jnp.right_shift(lane8, 3) == k, dk, wide)
        mean = [mean[g] + dk * Kf[g, 8 * k : 8 * k + 8, :] for g in range(3)]
    same = jnp.bitwise_and(jnp.right_shift(lane8, 1), 3) == jnp.right_shift(sub8, 1)
    for g in range(3):
        part = jnp.where(same, share[g : g + 1, :] * wide, 0.0)
        shift = jnp.broadcast_to(jnp.sum(part, axis=1, keepdims=True), (8, 256))
        mrow_out[8 * g : 8 * g + 8, :] = mean[g] - wet8 * shift
    for c in outs:
        c.wait()
    for c in sends:
        c.wait_send()


def local(ensemble, velocity, diffusivity, land_mask, obs_index, obs_owner, obs_value, obs_error):
    hbm = pl.BlockSpec(memory_space=pltpu.HBM)
    vm = lambda *shape, t=F32: pltpu.VMEM(shape, t)
    dma = lambda n: pltpu.SemaphoreType.DMA((n,))
    x1, mrow = pl.pallas_call(
        kernel,
        out_shape=(jax.ShapeDtypeStruct((80, 12, 2, 256), F32), jax.ShapeDtypeStruct((24, 256), F32)),
        in_specs=[hbm] * 8,
        out_specs=(pl.BlockSpec(memory_space=pl.ANY), pl.BlockSpec(memory_space=pltpu.VMEM)),
        scratch_shapes=[
            pltpu.SMEM((4,), F32), pltpu.SMEM((4, 4, 8), jnp.int32), pltpu.SMEM((4,), jnp.int32),
            pltpu.SMEM((4, 8), F32), pltpu.SMEM((4, 8), F32),
            vm(10, 12, 16, 256), vm(2, 3, 16, 256), vm(16, 256, t=jnp.int32), vm(10, 12, 16, 256),
            vm(20, 12, 8, 256), vm(12, 16, 128), vm(12, 16, 128), vm(2, 16, 128), vm(2, 2, 16, 128),
            vm(16, 128), vm(15, 16, 128), vm(8, 16, 128), vm(32, 32, 128), vm(32, 8, 256),
            vm(32, 128), vm(32, 128), vm(32, 128), vm(32, 128), vm(32, 32, 128),
            vm(256, 640, t=BF16), vm(256, 640, t=BF16), vm(640, 256, t=BF16), vm(640, 256, t=BF16),
            vm(3, 256, 256), vm(3, 256, 256, t=BF16), vm(3, 256, 256, t=BF16),
            vm(2, 8, 256), vm(15, 8, 256), vm(7, 8, 256),
            dma(10), dma(3), dma(24), dma(2), dma(2), dma(21), dma(21),
            dma(15), dma(15), dma(7), dma(7), dma(15), dma(15), dma(7), dma(7),
        ],
        compiler_params=pltpu.CompilerParams(collective_id=0, has_side_effects=True, vmem_limit_bytes=58 << 20),
    )(
        ensemble.reshape(10, 12, 16, 256),
        velocity,
        land_mask,
        diffusivity,
        jnp.transpose(obs_index, (0, 2, 1)),
        obs_owner,
        obs_value,
        obs_error,
    )
    return (x1 + mrow.reshape(1, 12, 2, 256)).reshape(80, 4, 3, 2, 256)


def solution(mesh):
    in_specs = (
        P("member", None, None, None, "domain"),
        P(None, None, None, "domain"),
        P(),
        P(None, "domain"),
        P(),
        P(),
        P(),
        P(),
    )
    out_specs = P(None, None, None, "member", "domain")
    return jax.shard_map(local, mesh=mesh, in_specs=in_specs, out_specs=out_specs, check_vma=False)
```

time: 1790 us -> 61.8 us (0.03); the launches traced: 1770 us -> 61.6 us
  other arithmetic: 727 us -> 2.95 us
  blocking collectives: 512 us -> 0 us
  local copies, waits for them, and re-layouts: 303 us -> 0.75 us
  between operations: 119 us -> 0.01 us
  matrix products: 96.1 us -> 0 us
  Pallas kernels: 0 us -> 57.9 us
    psum x8 -> x0, blocking collectives: 512 us -> none  [the longest x4 261 us: broadcast(): return lax.psum(kept, axis)]
    add x58 -> x1, other arithmetic: 385 us -> 2.95 us  [local(): return (x1 + mrow.reshape(1, 12, 2, 256)).reshape(80, 4, 3, 2, 256)]
    reduce_sum x72 -> x0, other arithmetic: 126 us -> none  [the longest x4 63.6 us: increment_sums(): per_cell = jnp.sum(change_flat.reshape(members, levels_total, -1), axis=0)]
    sub x39 -> x0, other arithmetic: 116 us -> none  [the longest x7 87.1 us: local(): flat_state.reshape(members, levels_total, -1)]
    add x28 -> x1, local copies, waits for them, and re-layouts: 110 us -> 0.75 us  [local(): return (x1 + mrow.reshape(1, 12, 2, 256)).reshape(80, 4, 3, 2, 256)]
    dot_general x60 -> x0, matrix products: 96.1 us -> none  [the longest x32 82.8 us: local(): covariance = jnp.dot(anomaly, flat_state, precision=lax.Precision.HIGHEST)]
    mul x105 -> x0, other arithmetic: 73.4 us -> none  [the longest x64 43 us: separation(): return jnp.sqrt((col_gap * col_gap + row_gap * row_gap).astype(jnp.float32))]
    unnamed x378 -> x0, local copies, waits for them, and re-layouts: 68.3 us -> none
  transfers between devices with their start and end apart: 3 -> 0, of which waited for: 0 -> 0; matrix products, arithmetic and copies ran while one was open for 7% -> 0% of each run, Pallas kernels for 0% -> 0%
where the time goes in v1:
time: 61.8 us; the launch traced here: 61.6 us
  Pallas kernels  57.9 us (94%)
  other arithmetic  2.95 us (5%)
  local copies, waits for them, and re-layouts  0.75 us (1%)
    pallas_call x1, Pallas kernels, local(): pl.pallas_call(kernel, out_shape=(jax.ShapeDtypeStruct((80, 12, 2, 256),...  57.9 us
    add x1, other arithmetic, local(): return (x1 + mrow.reshape(1, 12, 2, 256)).reshape(80, 4, 3, 2, 256)  2.95 us

profile of v1, /device:TPU:1, one launch (start us, length us, event | category | flops | bytes accessed | tf_op | source)
XLA Modules:
  0.0 61.6 jit_solution(18206607150526643668)
XLA Ops:
  0.0 57.9 %shard_map.82 = (f32[80,12,2,256]{3,2,1,0:T(2,128)}, f32[24,256]{1,0:T(8,128)}) custom-call(f32[10,12,16,256]{3,2,1,0:T(8,128)} %bitcast.6, f32[2,3,16,256]{3,2,1,0:T(8,128)} %vel.1, s32[16,256]{1,0:T(8,128)} %mask.1, f32[4]{0:T(128)} %diff_in.1, s32[4,4,8]{2,1,0:T(4,128)} %bitcast.10, s32[4]{0:T(128)} %oown_in.1, f32[4,8]{1,0:T(4,128)} %oval_in.1, ...), custom_call_target="tpu_custom_call" | custom-call | tf_op jit(solution)/shard_map/pallas_call | solution.py:361
  57.9 0.8 %add.10 = f32[12,2,256]{2,1,0:T(2,128)S(1)} reshape(f32[24,256]{1,0:T(8,128)} %get-tuple-element.8) | data formatting | bytes 49152 | tf_op jit(solution)/shard_map/add | solution.py:390
  58.7 2.9 %broadcast_add_fusion = f32[80,3,8,256]{3,2,1,0:T(8,128)} fusion(f32[80,3,8,256]{3,2,1,0:T(8,128)} %bitcast.8, f32[3,8,256]{2,1,0:T(8,128)S(1)} %bitcast.9), kind=kLoop, calls=%fused_computation | loop fusion | flops 491520 | bytes 3956736 | tf_op jit(solution)/shard_map/add | solution.py:390

commit v2 on v1

--- a/solution.py
+++ b/solution.py
@@ -50,9 +50,9 @@
 
 def kernel(
     ens, vel, mask, diff_in, oidx_in, oown_in, oval_in, oerr_in, x1_out, mrow_out,
-    diff, oidx, oown, oval, oerr, E, V, W, F, D, eW, eE, pack, halo, vbuf, vin, Z, RB, TP, Pm, Zi, bcol, gcol, LB,
-    L1h, L1l, L2h, L2l, Kf, Kh, Kl, sbuf, sin1, sin2,
-    in_sem, loc_sem, out_sem, hs, hr, as_, ar, d1s, d1r, m1s, m1r, d2s, d2r, m2s, m2r,
+    diff, oidx, oown, oval, oerr, E, V, W, F, D, pack, halo, corr, CR, vbuf, vin, Z, RB, TP, Pm, Zi, bcol, gcol, LB,
+    L1h, L1l, L2h, L2l, Kf, Kh, Kl, sbuf, sin1, sin2, M,
+    in_sem, loc_sem, out_sem, hs, hr, cs, cr, as_, ar, d1s, d1r, m1s, m1r, d2s, d2r, m2s, m2r,
 ):
     me, dom = lax.axis_index("member"), lax.axis_index("domain")
 
@@ -74,6 +74,11 @@
     wet = W[...].astype(F32)
     row, col = iota((16, 256), 0), iota((16, 256), 1)
     lane16 = iota((16, 128), 1)
+    even = jnp.bitwise_and(lane16, 1) == 0
+    slot_fl = jnp.right_shift(lane16, 1)
+    for _ in range(4):
+        slot_fl = jnp.where(slot_fl >= 12, slot_fl - 12, slot_fl)
+    slot_fl = jnp.where(lane16 < 120, slot_fl, -1)
 
     def interior(fl, acc):
         acc = list(acc)
@@ -82,26 +87,29 @@
         cen = wet * (1.0 - 4.0 * d)
         east, west = wet * (d - 0.5 * u), wet * (d + 0.5 * u)
         north, south = wet * (d - 0.5 * v), wet * (d + 0.5 * v)
-        eW[fl] = jnp.where(lane16 == 0, west[:, :128], 0.0)
-        eE[fl] = jnp.where(lane16 == 127, east[:, 128:], 0.0)
+        ours = slot_fl == fl
+        acc[2] = jnp.where(ours & even, jnp.broadcast_to(east[:, 255:256], (16, 128)), acc[2])
+        acc[2] = jnp.where(ours & ~even, jnp.broadcast_to(west[:, 0:1], (16, 128)), acc[2])
         east, west = jnp.where(col == 255, 0.0, east), jnp.where(col == 0, 0.0, west)
         north, south = jnp.where(row == 15, 0.0, north), jnp.where(row == 0, 0.0, south)
         for m in range(10):
             x = E[m, fl]
-            F[m, fl] = (
+            y = (
                 cen * x
                 + east * pltpu.roll(x, 255, 1)
                 + west * pltpu.roll(x, 1, 1)
                 + north * pltpu.roll(x, 15, 0)
                 + south * pltpu.roll(x, 1, 0)
             )
+            F[m, fl] = y
+            E[m, fl] = y
             slot = 2 * ((m % 5) * 12 + fl)
             edges = pltpu.roll(jnp.where(lane16 == 0, x[:, :128], x[:, 128:]), slot, 1)
             here = (lane16 == slot) | (lane16 == jnp.bitwise_and(slot + 127, 127))
             acc[m // 5] = jnp.where(here, edges, acc[m // 5])
         return tuple(acc)
 
-    acc = (jnp.zeros((16, 128), F32), jnp.zeros((16, 128), F32))
+    acc = tuple(jnp.zeros((16, 128), F32) for _ in range(3))
     for g in range(3):
         copies[g].wait()
         acc = lax.fori_loop(4 * g, 4 * g + 4, interior, acc)
@@ -154,44 +162,53 @@
 
     to_left = remote(pack, halo.at[0], hs.at[0], hr.at[0], {"domain": left})
     to_right = remote(pack, halo.at[1], hs.at[1], hr.at[1], {"domain": right})
-    to_left.wait_recv()
-    to_right.wait_recv()
-    even = jnp.bitwise_and(lane16, 1) == 0
-    merged = [jnp.where(even, halo[0, h], pltpu.roll(halo[1, h], 2, 1)) for h in range(2)]
-
-    def fix(fl, carry):
-        west, east = eW[fl], eE[fl]
-        for m in range(10):
-            slot = 2 * ((m % 5) * 12 + fl)
-            y = pltpu.roll(merged[m // 5], 127 - slot, 1)
-            F[m, fl, :, 0:128] = F[m, fl, :, 0:128] + y * west
-            F[m, fl, :, 128:256] = F[m, fl, :, 128:256] + y * east
-        return carry
 
     arrivals, locals_ = [], []
+    own_rows, own_slot = pl.ds(2 * me, 2), pl.ds(2 * lax.rem(me, 4), 2)
+    half = lax.div(me, 4)
 
     def scatter(g):
-        fls = pl.ds(4 * g, 4)
-        mine = D.at[pl.ds(10 * lax.div(me, 4), 10), fls, pl.ds(2 * lax.rem(me, 4), 2), :]
-        c = pltpu.make_async_copy(F.at[:, fls, pl.ds(2 * me, 2), :], mine, loc_sem.at[g])
+        fls = pl.ds(2 * g, 2)
+        mine = D.at[pl.ds(10 * half, 10), fls, own_slot, :]
+        c = pltpu.make_async_copy(F.at[:, fls, own_rows, :], mine, loc_sem.at[g])
         c.start()
         locals_.append(c)
         for i in (4, 5, 3, 2, 6, 1, 7):
             t = lax.rem(me + i, MEM)
-            arrivals.append(
-                remote(F.at[:, fls, pl.ds(2 * t, 2), :], mine, as_.at[7 * g + i - 1], ar.at[7 * g + i - 1], {"member": t})
-            )
-
-    lax.fori_loop(0, 4, fix, 0)
+            n = 7 * g + i - 1
+            arrivals.append(remote(F.at[:, fls, pl.ds(2 * t, 2), :], mine, as_.at[n], ar.at[n], {"member": t}))
+
     scatter(0)
-    lax.fori_loop(4, 12, fix, 0)
+    scatter(1)
+
+    to_left.wait_recv()
+    to_right.wait_recv()
+    for h in range(2):
+        corr[h] = jnp.where(even, halo[0, h], pltpu.roll(halo[1, h], 2, 1)) * acc[2]
+    fixes = []
+    mine = CR.at[half, :, own_slot, :]
+    own_corr = pltpu.make_async_copy(corr.at[:, own_rows, :], mine, loc_sem.at[6])
+    own_corr.start()
+    for i in (4, 5, 3, 2, 6, 1, 7):
+        t = lax.rem(me + i, MEM)
+        fixes.append(remote(corr.at[:, pl.ds(2 * t, 2), :], mine, cs.at[i - 1], cr.at[i - 1], {"member": t}))
+    added = [corr[0], corr[1]]
+
+    def fix(fl, carry):
+        for m in range(10):
+            y = pltpu.roll(added[m // 5], 127 - 2 * ((m % 5) * 12 + fl), 1)
+            E[m, fl, :, 0:128] = E[m, fl, :, 0:128] + jnp.where(lane16 == 0, y, 0.0)
+            E[m, fl, :, 128:256] = E[m, fl, :, 128:256] + jnp.where(lane16 == 127, y, 0.0)
+        return carry
+
+    lax.fori_loop(0, 12, fix, 0)
 
     pick = (iota((256, 128), 0) + dom * 256 == wide_l(col_l, 256)) & (iota((256, 128), 1) < 32)
     pick = jnp.where(pick, 1.0, 0.0).astype(BF16)
     at_row = jnp.bitwise_and(iota((160, 128), 0), 15) == wide_l(row_l, 160)
     got = jnp.zeros((160, 128), F32)
     for fl in range(12):
-        x = F[:, fl].reshape(160, 256)
+        x = E[:, fl].reshape(160, 256)
         hi = x.astype(BF16)
         rest = x - hi.astype(F32)
         mid, lo = halves(rest)
@@ -202,7 +219,6 @@
     tile_parts = [
         remote(vbuf, vin.at[i - 1], d1s.at[i - 1], d1r.at[i - 1], {"domain": lax.rem(dom + i, DOM)}) for i in range(1, DOM)
     ]
-    scatter(1)
     scatter(2)
     total = vbuf[...]
     for i, c in enumerate(tile_parts):
@@ -212,6 +228,9 @@
     groups = [
         remote(Z.at[me], Z.at[me], m1s.at[i - 1], m1r.at[i - 1], {"member": lax.rem(me + i, MEM)}) for i in range(1, MEM)
     ]
+    scatter(3)
+    scatter(4)
+    scatter(5)
     for c in groups:
         c.wait_recv()
 
@@ -264,10 +283,24 @@
     invT = jnp.transpose(jnp.concatenate([Zi[...], jnp.zeros((96, 128), F32)], axis=0))[:32]
 
     sums = jnp.zeros((8, 256), F32)
+    own_corr.wait()
+    for c in fixes:
+        c.wait_recv()
+    first, last = iota((8, 128), 1) == 0, iota((8, 128), 1) == 127
+
+    def amend(fl, carry):
+        for u in range(20):
+            y = pltpu.roll(CR[u // 10, u % 10 // 5], 127 - 2 * ((u % 5) * 12 + fl), 1)
+            D[u, fl, :, 0:128] = D[u, fl, :, 0:128] + jnp.where(first, y, 0.0)
+            D[u, fl, :, 128:256] = D[u, fl, :, 128:256] + jnp.where(last, y, 0.0)
+        return carry
+
     for g in range(3):
-        locals_[g].wait()
-        for c in arrivals[7 * g : 7 * g + 7]:
-            c.wait_recv()
+        for u in (2 * g, 2 * g + 1):
+            locals_[u].wait()
+            for c in arrivals[7 * u : 7 * u + 7]:
+                c.wait_recv()
+        lax.fori_loop(4 * g, 4 * g + 4, amend, 0)
         xh, xl = halves(D[:, 4 * g : 4 * g + 4].reshape(640, 256))
         cov = mm(L1h[...], xh) + (mm(L1h[...], xl) + mm(L1l[...], xh))
         gains = []
@@ -347,7 +380,11 @@
     for g in range(3):
         part = jnp.where(same, share[g : g + 1, :] * wide, 0.0)
         shift = jnp.broadcast_to(jnp.sum(part, axis=1, keepdims=True), (8, 256))
-        mrow_out[8 * g : 8 * g + 8, :] = mean[g] - wet8 * shift
+        M[8 * g : 8 * g + 8, :] = mean[g] - wet8 * shift
+    for fl in range(12):
+        c = pltpu.make_async_copy(M.at[pl.ds(2 * fl, 2), :], mrow_out.at[fl], out_sem.at[24 + fl])
+        c.start()
+        outs.append(c)
     for c in outs:
         c.wait()
     for c in sends:
@@ -360,20 +397,20 @@
     dma = lambda n: pltpu.SemaphoreType.DMA((n,))
     x1, mrow = pl.pallas_call(
         kernel,
-        out_shape=(jax.ShapeDtypeStruct((80, 12, 2, 256), F32), jax.ShapeDtypeStruct((24, 256), F32)),
+        out_shape=(jax.ShapeDtypeStruct((80, 12, 2, 256), F32), jax.ShapeDtypeStruct((12, 2, 256), F32)),
         in_specs=[hbm] * 8,
-        out_specs=(pl.BlockSpec(memory_space=pl.ANY), pl.BlockSpec(memory_space=pltpu.VMEM)),
+        out_specs=(pl.BlockSpec(memory_space=pl.ANY), pl.BlockSpec(memory_space=pl.ANY)),
         scratch_shapes=[
             pltpu.SMEM((4,), F32), pltpu.SMEM((4, 4, 8), jnp.int32), pltpu.SMEM((4,), jnp.int32),
             pltpu.SMEM((4, 8), F32), pltpu.SMEM((4, 8), F32),
             vm(10, 12, 16, 256), vm(2, 3, 16, 256), vm(16, 256, t=jnp.int32), vm(10, 12, 16, 256),
-            vm(20, 12, 8, 256), vm(12, 16, 128), vm(12, 16, 128), vm(2, 16, 128), vm(2, 2, 16, 128),
+            vm(20, 12, 8, 256), vm(2, 16, 128), vm(2, 2, 16, 128), vm(2, 16, 128), vm(2, 2, 8, 128),
             vm(16, 128), vm(15, 16, 128), vm(8, 16, 128), vm(32, 32, 128), vm(32, 8, 256),
             vm(32, 128), vm(32, 128), vm(32, 128), vm(32, 128), vm(32, 32, 128),
             vm(256, 640, t=BF16), vm(256, 640, t=BF16), vm(640, 256, t=BF16), vm(640, 256, t=BF16),
             vm(3, 256, 256), vm(3, 256, 256, t=BF16), vm(3, 256, 256, t=BF16),
-            vm(2, 8, 256), vm(15, 8, 256), vm(7, 8, 256),
-            dma(10), dma(3), dma(24), dma(2), dma(2), dma(21), dma(21),
+            vm(2, 8, 256), vm(15, 8, 256), vm(7, 8, 256), vm(24, 256),
+            dma(10), dma(7), dma(36), dma(2), dma(2), dma(7), dma(7), dma(42), dma(42),
             dma(15), dma(15), dma(7), dma(7), dma(15), dma(15), dma(7), dma(7),
         ],
         compiler_params=pltpu.CompilerParams(collective_id=0, has_side_effects=True, vmem_limit_bytes=58 << 20),
@@ -387,7 +424,7 @@
         obs_value,
         obs_error,
     )
-    return (x1 + mrow.reshape(1, 12, 2, 256)).reshape(80, 4, 3, 2, 256)
+    return (x1 + mrow[None]).reshape(80, 4, 3, 2, 256)
 
 
 def solution(mesh):

time: 61.8 us -> 53.8 us (0.87)
  Pallas kernels: 57.9 us -> 50.7 us
  local copies, waits for them, and re-layouts: 0.75 us -> 0 us
    pallas_call x1, Pallas kernels: 57.9 us -> 50.7 us  [local(): pl.pallas_call(kernel, out_shape=(jax.ShapeDtypeStruct((80, 12, 2, 256),...]
    add x1 -> x0, local copies, waits for them, and re-layouts: 0.75 us -> none  [local(): return (x1 + mrow.reshape(1, 12, 2, 256)).reshape(80, 4, 3, 2, 256)]
where the time goes in v2:
time: 53.8 us; the launch traced here: 53.6 us
  Pallas kernels  50.7 us (94%)
  other arithmetic  2.95 us (5%)
    pallas_call x1, Pallas kernels, local(): pl.pallas_call(kernel, out_shape=(jax.ShapeDtypeStruct((80, 12, 2, 256),...  50.7 us
    add x1, other arithmetic, local(): return (x1 + mrow[None]).reshape(80, 4, 3, 2, 256)  2.95 us

profile of v2, /device:TPU:1, one launch (start us, length us, event | category | flops | bytes accessed | tf_op | source)
XLA Modules:
  0.0 53.6 jit_solution(9726255276191418896)
XLA Ops:
  0.0 50.7 %shard_map.82 = (f32[80,12,2,256]{3,2,1,0:T(2,128)}, f32[12,2,256]{2,1,0:T(2,128)}) custom-call(f32[10,12,16,256]{3,2,1,0:T(8,128)} %bitcast.6, f32[2,3,16,256]{3,2,1,0:T(8,128)} %vel.1, s32[16,256]{1,0:T(8,128)} %mask.1, f32[4]{0:T(128)} %diff_in.1, s32[4,4,8]{2,1,0:T(4,128)} %bitcast.10, s32[4]{0:T(128)} %oown_in.1, f32[4,8]{1,0:T(4,128)} %oval_in.1, ...), custom_call_target="tpu_custom_call" | custom-call | tf_op jit(solution)/shard_map/pallas_call | solution.py:398
  50.7 2.9 %broadcast_add_fusion = f32[80,3,8,256]{3,2,1,0:T(8,128)} fusion(f32[80,3,8,256]{3,2,1,0:T(8,128)} %bitcast.8, f32[3,8,256]{2,1,0:T(8,128)} %bitcast.9), kind=kLoop, calls=%fused_computation | loop fusion | flops 491520 | bytes 3956736 | tf_op jit(solution)/shard_map/add | solution.py:427

commit v3 on v2

--- a/solution.py
+++ b/solution.py
@@ -7,6 +7,8 @@
 
 LOC_RADIUS = 64.0
 MEM, DOM = 8, 16
+FAR_FIRST = (5, 3, 7, 4, 1, 2, 6)
+NEAR_LAST = (5, 13, 3, 7, 11, 15, 12, 4, 1, 9, 10, 14, 2, 6, 8)
 MESH = pl.DeviceIdType.MESH
 F32, BF16 = jnp.float32, jnp.bfloat16
 HIGH = lax.Precision.HIGHEST
@@ -50,7 +52,7 @@
 
 def kernel(
     ens, vel, mask, diff_in, oidx_in, oown_in, oval_in, oerr_in, x1_out, mrow_out,
-    diff, oidx, oown, oval, oerr, E, V, W, F, D, pack, halo, corr, CR, vbuf, vin, Z, RB, TP, Pm, Zi, bcol, gcol, LB,
+    diff, oidx, oown, oval, oerr, E, V, W, F, D, pack, halo, corr, CR, vbuf, vtmp, vin, vin2, Z, RB, TP, Pm, Zi, bcol, gcol, LB,
     L1h, L1l, L2h, L2l, Kf, Kh, Kl, sbuf, sin1, sin2, M,
     in_sem, loc_sem, out_sem, hs, hr, cs, cr, as_, ar, d1s, d1r, m1s, m1r, d2s, d2r, m2s, m2r,
 ):
@@ -64,10 +66,18 @@
     for c in small + copies:
         c.start()
     barrier = pltpu.get_barrier_semaphore()
-    for i in range(1, MEM):
-        pl.semaphore_signal(barrier, inc=1, device_id={"member": lax.rem(me + i, MEM)}, device_id_type=MESH)
-    for i in range(1, DOM):
-        pl.semaphore_signal(barrier, inc=1, device_id={"domain": lax.rem(dom + i, DOM)}, device_id_type=MESH)
+    right, left = lax.rem(dom + 1, DOM), lax.rem(dom + DOM - 1, DOM)
+
+    def across(i):
+        return {"member": jnp.bitwise_xor(me, i % 8), "domain": jnp.bitwise_xor(dom, 8 * (i // 8))}
+
+    def along(i):
+        return {"domain": jnp.bitwise_xor(dom, i)}
+
+    for where in [across(i) for i in range(1, 16)] + [along(i) for i in range(1, 8)]:
+        pl.semaphore_signal(barrier, inc=1, device_id=where, device_id_type=MESH)
+    for where in (left, right):
+        pl.semaphore_signal(barrier, inc=1, device_id={"domain": where}, device_id_type=MESH)
     for c in small:
         c.wait()
 
@@ -94,15 +104,13 @@
         north, south = jnp.where(row == 15, 0.0, north), jnp.where(row == 0, 0.0, south)
         for m in range(10):
             x = E[m, fl]
-            y = (
+            F[m, fl] = (
                 cen * x
                 + east * pltpu.roll(x, 255, 1)
                 + west * pltpu.roll(x, 1, 1)
                 + north * pltpu.roll(x, 15, 0)
                 + south * pltpu.roll(x, 1, 0)
             )
-            F[m, fl] = y
-            E[m, fl] = y
             slot = 2 * ((m % 5) * 12 + fl)
             edges = pltpu.roll(jnp.where(lane16 == 0, x[:, :128], x[:, 128:]), slot, 1)
             here = (lane16 == slot) | (lane16 == jnp.bitwise_and(slot + 127, 127))
@@ -110,10 +118,44 @@
         return tuple(acc)
 
     acc = tuple(jnp.zeros((16, 128), F32) for _ in range(3))
-    for g in range(3):
+    copies[0].wait()
+    acc = lax.fori_loop(0, 4, interior, acc)
+
+    pl.semaphore_wait(barrier, 24)
+    sends = []
+
+    def remote(src, dst, send, recv, where):
+        c = pltpu.make_async_remote_copy(
+            src_ref=src, dst_ref=dst, send_sem=send, recv_sem=recv, device_id=where, device_id_type=MESH
+        )
+        c.start()
+        sends.append(c)
+        return c
+
+    arrivals, locals_ = [], []
+    own_rows, own_slot = pl.ds(2 * me, 2), pl.ds(2 * lax.rem(me, 4), 2)
+    half = lax.div(me, 4)
+
+    def scatter(g):
+        fls = pl.ds(g, 1)
+        mine = D.at[pl.ds(10 * half, 10), fls, own_slot, :]
+        c = pltpu.make_async_copy(F.at[:, fls, own_rows, :], mine, loc_sem.at[g])
+        c.start()
+        locals_.append(c)
+        for i in FAR_FIRST:
+            t = jnp.bitwise_xor(me, i)
+            n = 7 * g + i - 1
+            arrivals.append(remote(F.at[:, fls, pl.ds(2 * t, 2), :], mine, as_.at[n], ar.at[n], {"member": t}))
+
+    scatter(0)
+    scatter(1)
+    for g in (1, 2):
         copies[g].wait()
         acc = lax.fori_loop(4 * g, 4 * g + 4, interior, acc)
     pack[0], pack[1] = acc[0], acc[1]
+
+    to_left = remote(pack, halo.at[0], hs.at[0], hr.at[0], {"domain": left})
+    to_right = remote(pack, halo.at[1], hs.at[1], hr.at[1], {"domain": right})
 
     lane32, sub32 = iota((32, 128), 1), iota((32, 128), 0)
 
@@ -134,9 +176,65 @@
         row_s, col_s, fl_s = (jnp.where(sub32 == k, s, a) for s, a in ((r, row_s), (c, col_s), (f, fl_s)))
         row_l, col_l, fl_l = (jnp.where(lane32 == k, s, a) for s, a in ((r, row_l), (c, col_l), (f, fl_l)))
         val_s = jnp.where(sub32 == k, oval[b, n], val_s)
+    pick = (iota((256, 128), 0) + dom * 256 == wide_l(col_l, 256)) & (iota((256, 128), 1) < 32)
+    pick = jnp.where(pick, 1.0, 0.0).astype(BF16)
+    at_row = jnp.bitwise_and(iota((160, 128), 0), 15) == wide_l(row_l, 160)
+    got = jnp.zeros((160, 128), F32)
+    for fl in range(12):
+        x = F[:, fl].reshape(160, 256)
+        hi = x.astype(BF16)
+        rest = x - hi.astype(F32)
+        mid, lo = halves(rest)
+        got = jnp.where(wide_l(fl_l, 160) == fl, mm(hi, pick) + (mm(mid, pick) + mm(lo, pick)), got)
+    got = jnp.where(at_row, got, 0.0)
+    seen = jnp.sum(got.reshape(10, 16, 128), axis=1)
+    tile_l, edge_l = jnp.right_shift(col_l, 8), jnp.bitwise_and(col_l, 255)
+    some = lane32 < 32
+    at_last, at_first = some & (edge_l == 255), some & (edge_l == 0)
+    spot = jnp.where(at_first & (jnp.bitwise_and(tile_l + 15, 15) == dom), 2 * fl_l - 1, -1000)
+    spot = jnp.where(at_last & (jnp.bitwise_and(tile_l + 1, 15) == dom), 2 * fl_l, spot)
+    coef = jnp.where(at_first & (tile_l == dom), 2 * fl_l + 1, jnp.where(at_last & (tile_l == dom), 2 * fl_l, -1000))
+    spot, coef = wide_l(pltpu.roll(spot, 32, 1), 128), wide_l(pltpu.roll(coef, 64, 1), 128)
+    picks = [spot + 24 * u for u in range(5)]
+    picks = [jnp.where(p == -1, 127, p) for p in picks] + [coef]
+    picks = jnp.concatenate([jnp.where(iota((128, 128), 0) == p, 1.0, 0.0).astype(BF16) for p in picks], axis=1)
+    rest = jnp.concatenate([acc[0], acc[1], acc[2]], axis=0)
+    hi = rest.astype(BF16)
+    mid, lo = halves(rest - hi.astype(F32))
+    extra = mm(hi, picks) + (mm(mid, picks) + mm(lo, picks))
+    in_row = iota((16, 128), 0) == wide_l(pltpu.roll(row_l, 32, 1), 16)
+    in_row2 = iota((16, 128), 0) == wide_l(pltpu.roll(row_l, 64, 1), 16)
+    vtmp[...] = jnp.zeros((16, 128), F32)
+    for m in range(10):
+        part = extra[16 * (m // 5) : 16 * (m // 5) + 16, 128 * (m % 5) : 128 * (m % 5) + 128]
+        vtmp[m : m + 1, :] = seen[m : m + 1, :] + jnp.sum(jnp.where(in_row, part, 0.0), axis=0, keepdims=True)
+    part = jnp.sum(jnp.where(in_row2, extra[32:48, 640:768], 0.0), axis=0, keepdims=True)
+    high = pltpu.roll(vtmp[8:16, :], 64, 1)
+    vbuf[...] = vtmp[0:8, :] + jnp.where(iota((8, 128), 0) == 2, part, high)
+    parts_a = [
+        remote(vbuf, vin.at[i], d1s.at[i - 1], d1r.at[i - 1], across(i)) for i in NEAR_LAST
+    ]
+    for g in range(2, 4):
+        scatter(g)
+
+    to_left.wait_recv()
+    to_right.wait_recv()
+    for h in range(2):
+        corr[h] = jnp.where(even, halo[0, h], pltpu.roll(halo[1, h], 2, 1)) * acc[2]
+    fixes = []
+    mine = CR.at[half, :, own_slot, :]
+    own_corr = pltpu.make_async_copy(corr.at[:, own_rows, :], mine, loc_sem.at[12])
+    own_corr.start()
+    for i in FAR_FIRST:
+        t = jnp.bitwise_xor(me, i)
+        fixes.append(remote(corr.at[:, pl.ds(2 * t, 2), :], mine, cs.at[i - 1], cr.at[i - 1], {"member": t}))
+    for g in range(4, 12):
+        scatter(g)
+
     rho = gaspari(separation(row_s, col_s, row_l, col_l))
     for k in range(32):
         RB[k] = jnp.broadcast_to(rho[:, k : k + 1], (32, 128))
+
 
     sub8, lane8 = iota((8, 256), 0), iota((8, 256), 1)
     odd = jnp.bitwise_and(sub8, 1) == 1
@@ -147,95 +245,22 @@
     for k in range(32):
         TP[k] = gaspari(separation(row8, col8, places[k][0], places[k][1])) * wet8
 
-    pl.semaphore_wait(barrier, MEM + DOM - 2)
-
-    right, left = lax.rem(dom + 1, DOM), lax.rem(dom + DOM - 1, DOM)
-    sends = []
-
-    def remote(src, dst, send, recv, where):
-        c = pltpu.make_async_remote_copy(
-            src_ref=src, dst_ref=dst, send_sem=send, recv_sem=recv, device_id=where, device_id_type=MESH
-        )
-        c.start()
-        sends.append(c)
-        return c
-
-    to_left = remote(pack, halo.at[0], hs.at[0], hr.at[0], {"domain": left})
-    to_right = remote(pack, halo.at[1], hs.at[1], hr.at[1], {"domain": right})
-
-    arrivals, locals_ = [], []
-    own_rows, own_slot = pl.ds(2 * me, 2), pl.ds(2 * lax.rem(me, 4), 2)
-    half = lax.div(me, 4)
-
-    def scatter(g):
-        fls = pl.ds(2 * g, 2)
-        mine = D.at[pl.ds(10 * half, 10), fls, own_slot, :]
-        c = pltpu.make_async_copy(F.at[:, fls, own_rows, :], mine, loc_sem.at[g])
-        c.start()
-        locals_.append(c)
-        for i in (4, 5, 3, 2, 6, 1, 7):
-            t = lax.rem(me + i, MEM)
-            n = 7 * g + i - 1
-            arrivals.append(remote(F.at[:, fls, pl.ds(2 * t, 2), :], mine, as_.at[n], ar.at[n], {"member": t}))
-
-    scatter(0)
-    scatter(1)
-
-    to_left.wait_recv()
-    to_right.wait_recv()
-    for h in range(2):
-        corr[h] = jnp.where(even, halo[0, h], pltpu.roll(halo[1, h], 2, 1)) * acc[2]
-    fixes = []
-    mine = CR.at[half, :, own_slot, :]
-    own_corr = pltpu.make_async_copy(corr.at[:, own_rows, :], mine, loc_sem.at[6])
-    own_corr.start()
-    for i in (4, 5, 3, 2, 6, 1, 7):
-        t = lax.rem(me + i, MEM)
-        fixes.append(remote(corr.at[:, pl.ds(2 * t, 2), :], mine, cs.at[i - 1], cr.at[i - 1], {"member": t}))
-    added = [corr[0], corr[1]]
-
-    def fix(fl, carry):
-        for m in range(10):
-            y = pltpu.roll(added[m // 5], 127 - 2 * ((m % 5) * 12 + fl), 1)
-            E[m, fl, :, 0:128] = E[m, fl, :, 0:128] + jnp.where(lane16 == 0, y, 0.0)
-            E[m, fl, :, 128:256] = E[m, fl, :, 128:256] + jnp.where(lane16 == 127, y, 0.0)
-        return carry
-
-    lax.fori_loop(0, 12, fix, 0)
-
-    pick = (iota((256, 128), 0) + dom * 256 == wide_l(col_l, 256)) & (iota((256, 128), 1) < 32)
-    pick = jnp.where(pick, 1.0, 0.0).astype(BF16)
-    at_row = jnp.bitwise_and(iota((160, 128), 0), 15) == wide_l(row_l, 160)
-    got = jnp.zeros((160, 128), F32)
-    for fl in range(12):
-        x = E[:, fl].reshape(160, 256)
-        hi = x.astype(BF16)
-        rest = x - hi.astype(F32)
-        mid, lo = halves(rest)
-        got = jnp.where(wide_l(fl_l, 160) == fl, mm(hi, pick) + (mm(mid, pick) + mm(lo, pick)), got)
-    got = jnp.where(at_row, got, 0.0)
-    vbuf[...] = jnp.zeros((16, 128), F32)
-    vbuf[0:10, :] = jnp.sum(got.reshape(10, 16, 128), axis=1)
-    tile_parts = [
-        remote(vbuf, vin.at[i - 1], d1s.at[i - 1], d1r.at[i - 1], {"domain": lax.rem(dom + i, DOM)}) for i in range(1, DOM)
-    ]
-    scatter(2)
-    total = vbuf[...]
-    for i, c in enumerate(tile_parts):
+    for c in parts_a:
         c.wait_recv()
-        total = total + vin[i]
-    Z[me] = total
-    groups = [
-        remote(Z.at[me], Z.at[me], m1s.at[i - 1], m1r.at[i - 1], {"member": lax.rem(me + i, MEM)}) for i in range(1, MEM)
-    ]
-    scatter(3)
-    scatter(4)
-    scatter(5)
-    for c in groups:
+    vin[0] = vbuf[...]
+    for i in range(8):
+        Z[jnp.bitwise_xor(me, i)] = vin[i] + vin[i + 8]
+    parts_b = [remote(Z, vin2.at[i - 1], m1s.at[i - 1], m1r.at[i - 1], along(i)) for i in (4, 5, 2, 3, 6, 7, 1)]
+    for c in parts_b:
         c.wait_recv()
-
-    Y = jnp.transpose(Z[...].reshape(128, 128))[:32]
+    total = Z[...]
+    for i in range(7):
+        total = total + vin2[i]
+    total = jnp.concatenate([total, pltpu.roll(total, 64, 2)], axis=1)
+
+    Y = jnp.transpose(total.reshape(128, 128))
     real = jnp.bitwise_and(lane32, 15) < 10
+    Y = jnp.where(real, Y[0:32] + Y[32:64] * jnp.broadcast_to(Y[0:32, 10:11], (32, 128)), 0.0)
     ybar = jnp.broadcast_to(jnp.sum(Y, axis=1, keepdims=True) * (1.0 / 80.0), (32, 128))
     A = jnp.where(real, Y - ybar, 0.0)
     inv = jnp.where(lane32 == sub32, 1.0, 0.0).astype(F32)
@@ -296,7 +321,7 @@
         return carry
 
     for g in range(3):
-        for u in (2 * g, 2 * g + 1):
+        for u in range(4 * g, 4 * g + 4):
             locals_[u].wait()
             for c in arrivals[7 * u : 7 * u + 7]:
                 c.wait_recv()
@@ -319,8 +344,7 @@
         sums = sums + (mm_nt(pick, hi) + mm_nt(pick, lo))
     sbuf[0] = jnp.where(sub8 == 3, wet0 + wet1, sums)
     parts = [
-        remote(sbuf.at[0], sin1.at[i - 1], d2s.at[i - 1], d2r.at[i - 1], {"domain": lax.rem(dom + i, DOM)})
-        for i in range(1, DOM)
+        remote(sbuf.at[0], sin2.at[i - 1], m2s.at[i - 1], m2r.at[i - 1], along(i)) for i in (4, 5, 2, 3, 6, 7, 1)
     ]
 
     outs = []
@@ -340,18 +364,19 @@
     update(0)
     update(1)
     total = sbuf[0]
-    for i, c in enumerate(parts):
+    for c in parts:
         c.wait_recv()
-        total = total + sin1[i]
+    for i in range(7):
+        total = total + sin2[i]
     sbuf[1] = total
     parts = [
-        remote(sbuf.at[1], sin2.at[i - 1], m2s.at[i - 1], m2r.at[i - 1], {"member": lax.rem(me + i, MEM)})
-        for i in range(1, MEM)
+        remote(sbuf.at[1], sin1.at[i - 1], d2s.at[i - 1], d2r.at[i - 1], across(i)) for i in NEAR_LAST
     ]
     update(2)
-    for i, c in enumerate(parts):
+    for c in parts:
         c.wait_recv()
-        total = total + sin2[i]
+    for i in range(15):
+        total = total + sin1[i]
 
     cells = jnp.sum(jnp.sum(jnp.where(sub8 == 3, total, 0.0), axis=1, keepdims=True), axis=0, keepdims=True)
     share = total * (1.0 / jnp.broadcast_to(cells, (8, 256)))
@@ -405,12 +430,12 @@
             pltpu.SMEM((4, 8), F32), pltpu.SMEM((4, 8), F32),
             vm(10, 12, 16, 256), vm(2, 3, 16, 256), vm(16, 256, t=jnp.int32), vm(10, 12, 16, 256),
             vm(20, 12, 8, 256), vm(2, 16, 128), vm(2, 2, 16, 128), vm(2, 16, 128), vm(2, 2, 8, 128),
-            vm(16, 128), vm(15, 16, 128), vm(8, 16, 128), vm(32, 32, 128), vm(32, 8, 256),
+            vm(8, 128), vm(16, 128), vm(16, 8, 128), vm(7, 8, 8, 128), vm(8, 8, 128), vm(32, 32, 128), vm(32, 8, 256),
             vm(32, 128), vm(32, 128), vm(32, 128), vm(32, 128), vm(32, 32, 128),
             vm(256, 640, t=BF16), vm(256, 640, t=BF16), vm(640, 256, t=BF16), vm(640, 256, t=BF16),
             vm(3, 256, 256), vm(3, 256, 256, t=BF16), vm(3, 256, 256, t=BF16),
             vm(2, 8, 256), vm(15, 8, 256), vm(7, 8, 256), vm(24, 256),
-            dma(10), dma(7), dma(36), dma(2), dma(2), dma(7), dma(7), dma(42), dma(42),
+            dma(10), dma(13), dma(36), dma(2), dma(2), dma(7), dma(7), dma(84), dma(84),
             dma(15), dma(15), dma(7), dma(7), dma(15), dma(15), dma(7), dma(7),
         ],
         compiler_params=pltpu.CompilerParams(collective_id=0, has_side_effects=True, vmem_limit_bytes=58 << 20),

time: 53.8 us -> 50.8 us (0.944)
  Pallas kernels: 50.7 us -> 47.7 us
    pallas_call x1, Pallas kernels: 50.7 us -> 47.7 us  [local(): pl.pallas_call(kernel, out_shape=(jax.ShapeDtypeStruct((80, 12, 2, 256),...]
where the time goes in v3:
time: 50.8 us; the launch traced here: 50.6 us
  Pallas kernels  47.7 us (94%)
  other arithmetic  2.95 us (6%)
    pallas_call x1, Pallas kernels, local(): pl.pallas_call(kernel, out_shape=(jax.ShapeDtypeStruct((80, 12, 2, 256),...  47.7 us
    add x1, other arithmetic, local(): return (x1 + mrow[None]).reshape(80, 4, 3, 2, 256)  2.95 us

profile of v3, /device:TPU:1, one launch (start us, length us, event | category | flops | bytes accessed | tf_op | source)
XLA Modules:
  0.0 50.6 jit_solution(15478748987820232819)
XLA Ops:
  0.0 47.7 %shard_map.82 = (f32[80,12,2,256]{3,2,1,0:T(2,128)}, f32[12,2,256]{2,1,0:T(2,128)}) custom-call(f32[10,12,16,256]{3,2,1,0:T(8,128)} %bitcast.6, f32[2,3,16,256]{3,2,1,0:T(8,128)} %vel.1, s32[16,256]{1,0:T(8,128)} %mask.1, f32[4]{0:T(128)} %diff_in.1, s32[4,4,8]{2,1,0:T(4,128)} %bitcast.10, s32[4]{0:T(128)} %oown_in.1, f32[4,8]{1,0:T(4,128)} %oval_in.1, ...), custom_call_target="tpu_custom_call" | custom-call | tf_op jit(solution)/shard_map/pallas_call | solution.py:423
  47.7 2.9 %broadcast_add_fusion = f32[80,3,8,256]{3,2,1,0:T(8,128)} fusion(f32[80,3,8,256]{3,2,1,0:T(8,128)} %bitcast.8, f32[3,8,256]{2,1,0:T(8,128)} %bitcast.9), kind=kLoop, calls=%fused_computation | loop fusion | flops 491520 | bytes 3956736 | tf_op jit(solution)/shard_map/add | solution.py:452

commit v4 on v3

--- a/solution.py
+++ b/solution.py
@@ -53,7 +53,7 @@
 def kernel(
     ens, vel, mask, diff_in, oidx_in, oown_in, oval_in, oerr_in, x1_out, mrow_out,
     diff, oidx, oown, oval, oerr, E, V, W, F, D, pack, halo, corr, CR, vbuf, vtmp, vin, vin2, Z, RB, TP, Pm, Zi, bcol, gcol, LB,
-    L1h, L1l, L2h, L2l, Kf, Kh, Kl, sbuf, sin1, sin2, M,
+    L1h, L1l, L2h, L2l, Kf, Kh, Kl, sbuf, sin1, sin2, M, TQ, Kd,
     in_sem, loc_sem, out_sem, hs, hr, cs, cr, as_, ar, d1s, d1r, m1s, m1r, d2s, d2r, m2s, m2r,
 ):
     me, dom = lax.axis_index("member"), lax.axis_index("domain")
@@ -244,6 +244,9 @@
     row8, col8 = 2 * me + jnp.bitwise_and(sub8, 1), dom * 256 + lane8
     for k in range(32):
         TP[k] = gaspari(separation(row8, col8, places[k][0], places[k][1])) * wet8
+        for h in range(2):
+            taper = gaspari(separation(8 * h + sub8, col8, places[k][0], places[k][1]))
+            TQ[32 * h + k] = taper * W[8 * h : 8 * h + 8, :].astype(F32)
 
     for c in parts_a:
         c.wait_recv()
@@ -285,7 +288,10 @@
     for j in range(31):
         LB[j] = jnp.broadcast_to(low[:, j : j + 1], (32, 128))
     for k in range(32):
-        TP[k] = TP[k] * jnp.broadcast_to(gcol[k : k + 1, 0:1], (8, 256))
+        g_k = jnp.broadcast_to(gcol[k : k + 1, 0:1], (8, 256))
+        TP[k] = TP[k] * g_k
+        TQ[k] = TQ[k] * g_k
+        TQ[32 + k] = TQ[32 + k] * g_k
 
     n = iota((128, 640), 1)
     unit = jnp.right_shift(n, 5)
@@ -307,7 +313,54 @@
     L2l[...] = jnp.transpose(kron(lo)).astype(BF16)
     invT = jnp.transpose(jnp.concatenate([Zi[...], jnp.zeros((96, 128), F32)], axis=0))[:32]
 
-    sums = jnp.zeros((8, 256), F32)
+    def recursion(cov, taper, out):
+        gains = []
+        for k in range(32):
+            left_, right_ = cov[8 * k : 8 * k + 8, :128], cov[8 * k : 8 * k + 8, 128:]
+            for j in range(k):
+                s = jnp.broadcast_to(LB[j, k : k + 1, :], (8, 128))
+                left_, right_ = left_ - s * gains[j][0], right_ - s * gains[j][1]
+            t = taper(k)
+            left_, right_ = left_ * t[:, 0:128], right_ * t[:, 128:256]
+            gains.append((left_, right_))
+            out[8 * k : 8 * k + 8, 0:128] = left_
+            out[8 * k : 8 * k + 8, 128:256] = right_
+
+    added = [corr[0], corr[1]]
+
+    def amend_own(fl, carry):
+        for m in range(10):
+            y = pltpu.roll(added[m // 5], 127 - 2 * ((m % 5) * 12 + fl), 1)
+            E[m, fl, :, 0:128] = F[m, fl, :, 0:128] + jnp.where(lane16 == 0, y, 0.0)
+            E[m, fl, :, 128:256] = F[m, fl, :, 128:256] + jnp.where(lane16 == 127, y, 0.0)
+        return carry
+
+    lax.fori_loop(10, 12, amend_own, 0)
+    own = jnp.where(iota((128, 80), 0) == me * 16 + jnp.right_shift(iota((128, 80), 1), 3), 1.0, 0.0).astype(BF16)
+    keep_own = jnp.where(jnp.bitwise_and(iota((8, 80), 1), 7) == iota((8, 80), 0), 1.0, 0.0)
+    keep_own = jnp.broadcast_to(keep_own[None], (32, 8, 80))
+
+    def kron_own(part):
+        return (jnp.broadcast_to(mm(part, own)[:, None, :], (32, 8, 80)) * keep_own).reshape(256, 80).astype(BF16)
+
+    hi, lo = halves(Pv)
+    own_h, own_l = kron_own(hi), kron_own(lo)
+    group = jnp.right_shift(iota((256, 256), 0), 3) == jnp.right_shift(iota((256, 256), 1), 3)
+    group = jnp.where(group, 1.0, 0.0).astype(BF16)
+    third = jnp.where(sub8 == 2, 1.0, 0.0).astype(BF16)
+
+    def own_sums(u, acc):
+        f, h = jnp.right_shift(u, 1), jnp.bitwise_and(u, 1)
+        x = E[:, 8 + f, pl.ds(pl.multiple_of(8 * h, 8), 8), :]
+        xh, xl = halves(x.reshape(80, 256))
+        recursion(mm(own_h, xh) + (mm(own_h, xl) + mm(own_l, xh)), lambda k: TQ[32 * h + k], Kd)
+        kh, kl = halves(Kd[...])
+        th, tl = halves(mm_nt(third, kh) + mm_nt(third, kl))
+        here = (jnp.bitwise_and(jnp.right_shift(lane8, 1), 3) == f) & ~(jnp.bitwise_and(lane8, 1) == 1)
+        return acc + jnp.where(here, mm(th, group) + mm(tl, group), 0.0)
+
+    sums = lax.fori_loop(4, 8, own_sums, jnp.zeros((8, 256), F32))
+
     own_corr.wait()
     for c in fixes:
         c.wait_recv()
@@ -320,28 +373,30 @@
             D[u, fl, :, 128:256] = D[u, fl, :, 128:256] + jnp.where(last, y, 0.0)
         return carry
 
-    for g in range(3):
-        for u in range(4 * g, 4 * g + 4):
+    def arrive(first_fl, end_fl):
+        for u in range(first_fl, end_fl):
             locals_[u].wait()
             for c in arrivals[7 * u : 7 * u + 7]:
                 c.wait_recv()
-        lax.fori_loop(4 * g, 4 * g + 4, amend, 0)
+        lax.fori_loop(first_fl, end_fl, amend, 0)
+
+    def cell_gains(g):
+        arrive(4 * g if g < 2 else 10, 4 * g + 4)
         xh, xl = halves(D[:, 4 * g : 4 * g + 4].reshape(640, 256))
         cov = mm(L1h[...], xh) + (mm(L1h[...], xl) + mm(L1l[...], xh))
-        gains = []
-        for k in range(32):
-            left_, right_ = cov[8 * k : 8 * k + 8, :128], cov[8 * k : 8 * k + 8, 128:]
-            for j in range(k):
-                s = jnp.broadcast_to(LB[j, k : k + 1, :], (8, 128))
-                left_, right_ = left_ - s * gains[j][0], right_ - s * gains[j][1]
-            left_, right_ = left_ * TP[k, :, 0:128], right_ * TP[k, :, 128:256]
-            gains.append((left_, right_))
-            Kf[g, 8 * k : 8 * k + 8, 0:128] = left_
-            Kf[g, 8 * k : 8 * k + 8, 128:256] = right_
+        recursion(cov, lambda k: TP[k], Kf.at[g])
         hi, lo = halves(Kf[g])
         Kh[g], Kl[g] = hi, lo
         pick = jnp.where(sub8 == g, 1.0, 0.0).astype(BF16)
-        sums = sums + (mm_nt(pick, hi) + mm_nt(pick, lo))
+        return mm_nt(pick, hi) + mm_nt(pick, lo)
+
+    for g in range(2):
+        sums = sums + cell_gains(g)
+    arrive(8, 10)
+    xh, xl = halves(jnp.concatenate([D[:, 8:10], jnp.zeros((20, 2, 8, 256), F32)], axis=1).reshape(640, 256))
+    recursion(mm(L1h[...], xh) + (mm(L1h[...], xl) + mm(L1l[...], xh)), lambda k: TP[k], Kd)
+    hi, lo = halves(Kd[...])
+    sums = sums + (mm_nt(third, hi) + mm_nt(third, lo))
     sbuf[0] = jnp.where(sub8 == 3, wet0 + wet1, sums)
     parts = [
         remote(sbuf.at[0], sin2.at[i - 1], m2s.at[i - 1], m2r.at[i - 1], along(i)) for i in (4, 5, 2, 3, 6, 7, 1)
@@ -362,7 +417,6 @@
             outs.append(c)
 
     update(0)
-    update(1)
     total = sbuf[0]
     for c in parts:
         c.wait_recv()
@@ -372,6 +426,8 @@
     parts = [
         remote(sbuf.at[1], sin1.at[i - 1], d2s.at[i - 1], d2r.at[i - 1], across(i)) for i in NEAR_LAST
     ]
+    update(1)
+    cell_gains(2)
     update(2)
     for c in parts:
         c.wait_recv()
@@ -434,7 +490,7 @@
             vm(32, 128), vm(32, 128), vm(32, 128), vm(32, 128), vm(32, 32, 128),
             vm(256, 640, t=BF16), vm(256, 640, t=BF16), vm(640, 256, t=BF16), vm(640, 256, t=BF16),
             vm(3, 256, 256), vm(3, 256, 256, t=BF16), vm(3, 256, 256, t=BF16),
-            vm(2, 8, 256), vm(15, 8, 256), vm(7, 8, 256), vm(24, 256),
+            vm(2, 8, 256), vm(15, 8, 256), vm(7, 8, 256), vm(24, 256), vm(64, 8, 256), vm(256, 256),
             dma(10), dma(13), dma(36), dma(2), dma(2), dma(7), dma(7), dma(84), dma(84),
             dma(15), dma(15), dma(7), dma(7), dma(15), dma(15), dma(7), dma(7),
         ],

time: 50.8 us -> 50.4 us (level)
  no operation moved by 1% of the time
where the time goes in v4:
time: 50.4 us; the launch traced here: 50.3 us
  Pallas kernels  47.3 us (94%)
  other arithmetic  2.95 us (6%)
    pallas_call x1, Pallas kernels, local(): pl.pallas_call(kernel, out_shape=(jax.ShapeDtypeStruct((80, 12, 2, 256),...  47.3 us
    add x1, other arithmetic, local(): return (x1 + mrow[None]).reshape(80, 4, 3, 2, 256)  2.95 us

profile of v4, /device:TPU:1, one launch (start us, length us, event | category | flops | bytes accessed | tf_op | source)
XLA Modules:
  0.0 50.3 jit_solution(14043277850404701179)
XLA Ops:
  0.0 47.3 %shard_map.82 = (f32[80,12,2,256]{3,2,1,0:T(2,128)}, f32[12,2,256]{2,1,0:T(2,128)}) custom-call(f32[10,12,16,256]{3,2,1,0:T(8,128)} %bitcast.6, f32[2,3,16,256]{3,2,1,0:T(8,128)} %vel.1, s32[16,256]{1,0:T(8,128)} %mask.1, f32[4]{0:T(128)} %diff_in.1, s32[4,4,8]{2,1,0:T(4,128)} %bitcast.10, s32[4]{0:T(128)} %oown_in.1, f32[4,8]{1,0:T(4,128)} %oval_in.1, ...), custom_call_target="tpu_custom_call" | custom-call | tf_op jit(solution)/shard_map/pallas_call | solution.py:479
  47.3 2.9 %broadcast_add_fusion = f32[80,3,8,256]{3,2,1,0:T(8,128)} fusion(f32[80,3,8,256]{3,2,1,0:T(8,128)} %bitcast.8, f32[3,8,256]{2,1,0:T(8,128)} %bitcast.9), kind=kLoop, calls=%fused_computation | loop fusion | flops 491520 | bytes 3956736 | tf_op jit(solution)/shard_map/add | solution.py:508

commit v5 on v3

--- a/solution.py
+++ b/solution.py
@@ -214,7 +214,7 @@
     parts_a = [
         remote(vbuf, vin.at[i], d1s.at[i - 1], d1r.at[i - 1], across(i)) for i in NEAR_LAST
     ]
-    for g in range(2, 4):
+    for g in range(2, 5):
         scatter(g)
 
     to_left.wait_recv()
@@ -228,7 +228,7 @@
     for i in FAR_FIRST:
         t = jnp.bitwise_xor(me, i)
         fixes.append(remote(corr.at[:, pl.ds(2 * t, 2), :], mine, cs.at[i - 1], cr.at[i - 1], {"member": t}))
-    for g in range(4, 12):
+    for g in range(5, 12):
         scatter(g)
 
     rho = gaspari(separation(row_s, col_s, row_l, col_l))

time: 50.8 us -> 50.8 us (level)
  no operation moved by 1% of the time
where the time goes in v5:
time: 50.8 us; the launch traced here: 50.6 us
  Pallas kernels  47.7 us (94%)
  other arithmetic  2.95 us (6%)
    pallas_call x1, Pallas kernels, local(): pl.pallas_call(kernel, out_shape=(jax.ShapeDtypeStruct((80, 12, 2, 256),...  47.7 us
    add x1, other arithmetic, local(): return (x1 + mrow[None]).reshape(80, 4, 3, 2, 256)  2.95 us

profile of v5, /device:TPU:1, one launch (start us, length us, event | category | flops | bytes accessed | tf_op | source)
XLA Modules:
  0.0 50.6 jit_solution(11996389108271582417)
XLA Ops:
  0.0 47.7 %shard_map.82 = (f32[80,12,2,256]{3,2,1,0:T(2,128)}, f32[12,2,256]{2,1,0:T(2,128)}) custom-call(f32[10,12,16,256]{3,2,1,0:T(8,128)} %bitcast.6, f32[2,3,16,256]{3,2,1,0:T(8,128)} %vel.1, s32[16,256]{1,0:T(8,128)} %mask.1, f32[4]{0:T(128)} %diff_in.1, s32[4,4,8]{2,1,0:T(4,128)} %bitcast.10, s32[4]{0:T(128)} %oown_in.1, f32[4,8]{1,0:T(4,128)} %oval_in.1, ...), custom_call_target="tpu_custom_call" | custom-call | tf_op jit(solution)/shard_map/pallas_call | solution.py:423
  47.7 2.9 %broadcast_add_fusion = f32[80,3,8,256]{3,2,1,0:T(8,128)} fusion(f32[80,3,8,256]{3,2,1,0:T(8,128)} %bitcast.8, f32[3,8,256]{2,1,0:T(8,128)} %bitcast.9), kind=kLoop, calls=%fused_computation | loop fusion | flops 491520 | bytes 3956736 | tf_op jit(solution)/shard_map/add | solution.py:452
